TPU v7x, 128 devices: a whole 4x4x4 slice. The times are simulated.
128 devices in a mesh: gx: 8 (over z, core), yz: 16 (over x, y).
Axes of the slice: x: 4, y: 4, z: 4, core: 2. Of those that a mesh axis runs over, the one named last changes fastest.
Arguments:
- residual: bfloat16 [512, 18432], P('yz', 'gx'), may hold values from -1000 to 1000
- norm_gain: float32 [18432], P('gx'), may hold values from 0.1 to 1.9
- query_weight: bfloat16 [18432, 12288], P('gx', 'yz'), may hold values from -1 to 1
- kv_weight: bfloat16 [18432, 512], P('gx', 'yz'), may hold values from -1 to 1
- cache: bfloat16 [512, 2048, 512], P(('gx', 'yz')), may hold values from -1000 to 1000
- ffn_hidden: bfloat16 [512, 36864], P('gx', 'yz'), may hold values from -3 to 3
- out_weight: bfloat16 [12288, 18432], P('yz', 'gx'), may hold values from -0.0546875 to 0.0546875
- down_weight: bfloat16 [36864, 18432], P('yz', 'gx'), may hold values from -0.03125 to 0.03125
Outputs:
- update: bfloat16 [512, 18432], P('yz', 'gx')
All inputs are finite; a program needn't handle non-finite values.
Results may differ from a plain program's by a relative error of at most 0.02.
Values may be sent and summed in bfloat16 or wider, within the bound.
No kernel may reach another device: no remote copies, remote signals or barrier semaphores. Data moves between devices by JAX's collectives and lax.ppermute only.
A program may use at most 128 MiB of HBM per device.

v0:
```python
import jax
import jax.numpy as jnp
from jax import lax
from jax.sharding import PartitionSpec as P

D = 18432
HEADS = 48
HEAD = 256


def normalize(values, sums, squares, gain):
    mean = sums / D
    var = squares / D - mean * mean
    return ((values - mean[:, None]) * lax.rsqrt(var + 1e-05)[:, None] * gain[None, :]).astype(
        jnp.bfloat16
    )


def attend(query, fresh, cache):
    scale = HEAD ** (-0.5)
    scores = (
        jnp.einsum("rhd,rsd->rhs", query, cache[:, :, :HEAD], preferred_element_type=jnp.float32)
        * scale
    )
    own = (
        jnp.einsum("rhd,rd->rh", query, fresh[:, :HEAD], preferred_element_type=jnp.float32) * scale
    )
    highest = jnp.maximum(jnp.max(scores, axis=2), own)
    e_past = jnp.exp(scores - highest[:, :, None])
    e_own = jnp.exp(own - highest)
    total = jnp.sum(e_past, axis=2) + e_own
    w_past = (e_past / total[:, :, None]).astype(jnp.bfloat16)
    w_own = (e_own / total).astype(jnp.bfloat16)
    result = jnp.einsum(
        "rhs,rsd->rhd", w_past, cache[:, :, HEAD:], preferred_element_type=jnp.float32
    )
    result = result + w_own.astype(jnp.float32)[:, :, None] * fresh[:, None, HEAD:].astype(
        jnp.float32
    )
    return result.astype(jnp.bfloat16)


def body(residual, norm_gain, query_weight, kv_weight, cache, ffn_hidden, out_weight, down_weight):
    query_cols = query_weight.shape[1]
    fresh_cols = kv_weight.shape[1]
    yz_count = lax.axis_size("yz")
    whole_rows = lax.all_gather(residual, "yz", axis=0, tiled=True)
    values = whole_rows.astype(jnp.float32)
    sums, squares = lax.psum((jnp.sum(values, axis=1), jnp.sum(values * values, axis=1)), "gx")
    gathered = normalize(values, sums, squares, norm_gain)
    rows_here = gathered.shape[0] // lax.axis_size("gx")
    local_rows = rows_here // yz_count
    query_term = jnp.dot(gathered, query_weight, preferred_element_type=jnp.float32)
    fresh_term = jnp.dot(gathered, kv_weight, preferred_element_type=jnp.float32)
    summed = lax.psum_scatter(
        jnp.concatenate([query_term, fresh_term], axis=1), "gx", scatter_dimension=0, tiled=True
    ).astype(jnp.bfloat16)
    query_part = summed[:, :query_cols].reshape(yz_count, local_rows, query_cols)
    fresh_part = summed[:, query_cols:].reshape(yz_count, local_rows, fresh_cols)
    query_all, fresh_all = (
        lax.all_to_all(query_part, "yz", split_axis=0, concat_axis=2, tiled=True),
        lax.all_to_all(fresh_part, "yz", split_axis=0, concat_axis=2, tiled=True),
    )
    query = query_all.reshape(local_rows, HEADS, HEAD)
    fresh = fresh_all.reshape(local_rows, 2 * HEAD)
    attended = attend(query, fresh, cache).reshape(local_rows, yz_count, query_cols)
    back_heads = lax.all_to_all(attended, "yz", split_axis=1, concat_axis=0, tiled=True).reshape(
        rows_here, query_cols
    )
    joined = jnp.concatenate([back_heads, ffn_hidden], axis=1)
    piece = lax.all_gather(joined, "gx", axis=0, tiled=True)
    first = jnp.dot(piece[:, :query_cols], out_weight, preferred_element_type=jnp.float32)
    joint_terms = first + jnp.dot(
        piece[:, query_cols:], down_weight, preferred_element_type=jnp.float32
    )
    update = lax.psum_scatter(
        joint_terms.astype(jnp.bfloat16), "yz", scatter_dimension=0, tiled=True
    )
    return update


def solution(mesh):
    placed = (
        P("yz", "gx"),
        P("gx"),
        P("gx", "yz"),
        P("gx", "yz"),
        P(("gx", "yz"), None, None),
        P("gx", "yz"),
        P("yz", "gx"),
        P("yz", "gx"),
    )
    return jax.shard_map(body, mesh=mesh, in_specs=placed, out_specs=P("yz", "gx"), check_vma=False)
```

profile of v0, /device:TPU:0, one launch (start us, length us, event | category | flops | bytes accessed | tf_op | source)
XLA Modules:
  0.0 286.8 jit_solution(3322464609596382472)
XLA Ops:
  6.5 0.0 copy-start
  6.5 0.0 all-gather.3.cloned.1.call-start
  6.5 0.7 all-gather.3.cloned.1.call-update
  7.3 0.0 reduce-scatter.3.cloned.1.call-start
  7.3 50.4 %all-gather.3.cloned.1.call-done = bf16[512,2304]{1,0:T(8,128)(2,1)} async-done(((bf16[32,2304]{1,0:T(8,128)(2,1)}), bf16[512,2304]{1,0:T(8,128)(2,1)}) %all-gather.3.cloned.1.call-update) | async-done | bytes 2359312 | tf_op jit(solution)/shard_map/all_gather | solution.py:47
  57.7 2.5 convert_reduce_fusion
  60.2 13.8 %all-reduce = (f32[512]{0:T(512)S(1)}, f32[512]{0:T(512)S(1)}) all-reduce(f32[512]{0:T(512)S(1)} %get-tuple-element.6, f32[512]{0:T(512)S(1)} %get-tuple-element.5), channel_id=1, replica_groups=mesh['gx'=8,'yz'=16] {'gx'}, use_global_device_ids=true, to_apply=%region_3.0 | all-reduce | flops 1024 | bytes 8192 | tf_op jit(solution)/shard_map/psum | solution.py:49
  74.0 2.6 fusion.2
  76.5 0.0 copy-done.4
  76.5 0.7 fusion.30
  77.3 0.0 copy-done.3
  77.3 2.0 fusion.29
  79.3 1.4 pad_maximum_fusion
  80.7 0.0 reduce-scatter.3.cloned.1.call-update
  80.7 30.2 %reduce-scatter.3.cloned.1.call-done = f32[64,800]{1,0:T(8,128)} async-done(((f32[512,800]{1,0:T(8,128)}), f32[64,800]{1,0:T(8,128)}) %reduce-scatter.3.cloned.1.call-update) | async-done | bytes 204816 | tf_op jit(solution)/shard_map/reduce_scatter | solution.py:55
  110.9 1.0 convert_element_type.30
  111.9 0.0 copy-start.1
  111.9 0.6 copy-done.1
  112.5 0.6 slice.33
  113.1 6.8 %all-to-all-start.1 = ((bf16[16,4,32]{2,1,0:T(4,128)(2,1)}), bf16[16,4,32]{2,1,0:T(4,128)(2,1)S(1)}, u32[]{:S(2)}, u32[]{:S(2)}) async-start(bf16[16,4,32]{2,1,0:T(4,128)(2,1)} %bitcast.30), calls=%async_computation.2 | async-start | bytes 32768 | tf_op jit(solution)/shard_map/all_to_all | solution.py:62
  119.9 1.5 slice.32
  121.5 1.6 reshape.29
  123.0 4.5 %all-to-all-done.1 = bf16[16,4,32]{2,1,0:T(4,128)(2,1)S(1)} async-done(((bf16[16,4,32]{2,1,0:T(4,128)(2,1)}), bf16[16,4,32]{2,1,0:T(4,128)(2,1)S(1)}, u32[]{:S(2)}, u32[]{:S(2)}) %all-to-all-start.1) | async-done | bytes 4128 | tf_op jit(solution)/shard_map/all_to_all | solution.py:62
  127.5 4.2 %all-to-all-start = ((bf16[16,4,768]{2,1,0:T(4,128)(2,1)}), bf16[16,4,768]{2,1,0:T(4,128)(2,1)}, u32[]{:S(2)}, u32[]{:S(2)}) async-start(bf16[16,4,768]{2,1,0:T(4,128)(2,1)} %reshape.29), calls=%async_computation.1 | async-start | bytes 196608 | tf_op jit(solution)/shard_map/all_to_all | solution.py:61
  131.7 0.0 all-gather.5.cloned.1.call-start
  131.8 0.0 copy-done.2
  131.8 0.7 copy.18
  132.5 0.7 reshape.32
  133.2 0.7 slice_convert_fusion
  133.9 5.6 %all-to-all-done = bf16[16,4,768]{2,1,0:T(4,128)(2,1)} async-done(((bf16[16,4,768]{2,1,0:T(4,128)(2,1)}), bf16[16,4,768]{2,1,0:T(4,128)(2,1)}, u32[]{:S(2)}, u32[]{:S(2)}) %all-to-all-start) | async-done | bytes 98336 | tf_op jit(solution)/shard_map/all_to_all | solution.py:61
  139.5 1.5 copy.17
  141.0 1.6 reshape.30
  142.6 1.0 fusion.24
  143.6 3.7 %fusion.28 = (f32[4,48]{1,0:T(4,128)S(1)}, f32[4,48,2048]{2,1,0:T(8,128)S(1)}) fusion(bf16[4,48,256]{2,1,0:T(8,128)(2,1)} %reshape.30, bf16[4,2048,512]{2,1,0:T(8,128)(2,1)} %param.12), kind=kOutput, calls=%fused_computation.37 | convolution fusion | flops 202112832 | bytes 5866240 | tf_op jit(solution)/shard_map/rhd,rsd->rhs/dot_general | solution.py:22
  147.3 0.4 fusion.14
  147.7 3.7 %fusion.18 = bf16[4,48,256]{2,1,0:T(8,128)(2,1)} fusion(bf16[4,2048,512]{2,1,0:T(8,128)(2,1)} %param.12, f32[4,48,2048]{2,1,0:T(8,128)S(1)} %get-tuple-element.16, f32[4,48]{1,0:T(4,128)S(1)} %get-tuple-element.10, f32[4,48]{1,0:T(4,128)S(1)} %multiply_maximum_fusion, f32[4,256]{1,0:T(4,128)S(1)} %get-tuple-element.11, f32[4,48]{1,0:T(4,128)S(1)} %get-tuple-element.9), kind=kOutput, calls=%fused_computation.21 | convolution fusion | flops 202653696 | bytes 5871872 | tf_op jit(solution)/shard_map/rhs,rsd->rhd/dot_general | solution.py:34
  151.4 1.6 reshape.33
  153.0 0.9 copy.19
  153.9 11.2 %all_to_all.45 = bf16[4,16,768]{2,0,1:T(4,128)(2,1)} all-to-all(bf16[4,16,768]{2,0,1:T(4,128)(2,1)S(1)} %copy.19), channel_id=1, replica_groups=mesh['gx'=8,'yz'=16] {'yz'}, dimensions={1} | all-to-all | bytes 196608 | tf_op jit(solution)/shard_map/all_to_all | solution.py:67
  165.1 1.6 reshape.34
  166.7 1.7 pad_maximum_fusion.1
  168.5 0.0 all-gather.5.cloned.1.call-update
  168.5 0.0 reduce-scatter.5.cloned.1.call-start
  168.5 23.5 %all-gather.5.cloned.1.call-done = bf16[512,3072]{1,0:T(8,128)(2,1)} async-done(((bf16[64,3072]{1,0:T(8,128)(2,1)}), bf16[512,3072]{1,0:T(8,128)(2,1)}) %all-gather.5.cloned.1.call-update) | async-done | bytes 3145744 | tf_op jit(solution)/shard_map/all_gather | solution.py:71
  192.0 8.8 %fusion.12 = f32[512,2304]{1,0:T(8,128)S(1)} fusion(bf16[2304,2304]{1,0:T(8,128)(2,1)} %param.15, bf16[512,3072]{1,0:T(8,128)(2,1)} %all-gather.5.cloned.1.call-done), kind=kOutput, calls=%fused_computation.14 | convolution fusion | flops 5435817984 | bytes 17694720 | tf_op jit(solution)/shard_map/dot_general | solution.py:73
  200.8 4.6 %fusion.4 = bf16[512,2304]{1,0:T(8,128)(2,1)} fusion(f32[512,2304]{1,0:T(8,128)S(1)} %fusion.12, bf16[768,2304]{1,0:T(8,128)(2,1)S(1)} %copy-done, bf16[512,3072]{1,0:T(8,128)(2,1)} %all-gather.5.cloned.1.call-done), kind=kOutput, calls=%fused_computation.8 | convolution fusion | flops 1814298624 | bytes 11403264 | tf_op jit(solution)/shard_map/dot_general | solution.py:72
  205.4 0.0 reduce-scatter.5.cloned.1.call-update
  205.5 74.8 %reduce-scatter.5.cloned.1.call-done = bf16[32,2304]{1,0:T(8,128)(2,1)} async-done(((bf16[512,2304]{1,0:T(8,128)(2,1)}), bf16[32,2304]{1,0:T(8,128)(2,1)}) %reduce-scatter.5.cloned.1.call-update) | async-done | bytes 147472 | tf_op jit(solution)/shard_map/reduce_scatter | solution.py:76
  (7 shorter events, 0.0 us)
Async XLA Ops:
  6.5 194.3 %copy-start = (bf16[768,2304]{1,0:T(8,128)(2,1)S(1)}, bf16[768,2304]{1,0:T(8,128)(2,1)}, u32[]{:S(2)}) copy-start(bf16[768,2304]{1,0:T(8,128)(2,1)} %param.14) | copy-start | bytes 10616836
  6.5 51.2 %all-gather.3.cloned.1.call-start = ((), (), s32[]{:S(2)}) async-start(), calls=%async_computation.5 | async-start | bytes 2506752 | tf_op jit(solution)/shard_map/all_gather | solution.py:47
  7.3 103.6 %reduce-scatter.3.cloned.1.call-start = ((), (), s32[]{:S(2)}) async-start(), calls=%async_computation.6 | async-start | bytes 2064384 | tf_op jit(solution)/shard_map/reduce_scatter | solution.py:55
  73.9 2.6 copy-start.4
  73.9 3.4 %copy-start.3 = (bf16[2304,768]{1,0:T(8,128)(2,1)S(1)}, bf16[2304,768]{1,0:T(8,128)(2,1)}, u32[]{:S(2)}) copy-start(bf16[2304,768]{1,0:T(8,128)(2,1)} %param.10) | copy-start | bytes 10616836
  111.9 0.6 copy-start.1
  113.1 14.4 %all-to-all-start.1 = ((bf16[16,4,32]{2,1,0:T(4,128)(2,1)}), bf16[16,4,32]{2,1,0:T(4,128)(2,1)S(1)}, u32[]{:S(2)}, u32[]{:S(2)}) async-start(bf16[16,4,32]{2,1,0:T(4,128)(2,1)} %bitcast.30), calls=%async_computation.2 | async-start | bytes 32768 | tf_op jit(solution)/shard_map/all_to_all | solution.py:62
  127.5 4.2 %copy-start.2 = (bf16[16,4,32]{2,1,0:T(4,128)(2,1)}, bf16[16,4,32]{2,1,0:T(4,128)(2,1)S(1)}, u32[]{:S(2)}) copy-start(bf16[16,4,32]{2,1,0:T(4,128)(2,1)S(1)} %all-to-all-done.1) | copy-start | bytes 12292
  127.5 11.9 %all-to-all-start = ((bf16[16,4,768]{2,1,0:T(4,128)(2,1)}), bf16[16,4,768]{2,1,0:T(4,128)(2,1)}, u32[]{:S(2)}, u32[]{:S(2)}) async-start(bf16[16,4,768]{2,1,0:T(4,128)(2,1)} %reshape.29), calls=%async_computation.1 | async-start | bytes 196608 | tf_op jit(solution)/shard_map/all_to_all | solution.py:61
  131.7 60.3 %all-gather.5.cloned.1.call-start = ((), (), s32[]{:S(2)}) async-start(), calls=%async_computation.7 | async-start | bytes 3538944 | tf_op jit(solution)/shard_map/all_gather | solution.py:71
  168.5 111.8 %reduce-scatter.5.cloned.1.call-start = ((), (), s32[]{:S(2)}) async-start(), calls=%async_computation.8 | async-start | bytes 2506752 | tf_op jit(solution)/shard_map/reduce_scatter | solution.py:76
Sparse Core Ops, SparseCore 0:
  9.5 48.1 all-gather.2
  80.8 30.0 reduce-scatter.2
  168.6 23.3 all-gather.4
  205.6 74.6 reduce-scatter.4
where the time goes:
time: 288 us; the launch traced here: 287 us
  waiting for transfers between devices  190 us (66%)
  blocking collectives  25 us (9%)
  matrix products  24.6 us (9%)
  between operations  13.2 us (5%)
  local copies, waits for them, and re-layouts  13 us (5%)
  starting transfers between devices  11.1 us (4%)
  other arithmetic  10.2 us (4%)
    reduce_scatter x1, waiting for transfers between devices, body(): lax.psum_scatter(joint_terms.astype(jnp.bfloat16), 'yz', scatter_dimensio...  74.8 us
    all_gather x1, waiting for transfers between devices, body(): whole_rows = lax.all_gather(residual, 'yz', axis=0, tiled=True)  50.4 us
    reduce_scatter x1, waiting for transfers between devices, body(): lax.psum_scatter(jnp.concatenate([query_term, fresh_term], axis=1), 'gx',...  30.2 us
    all_gather x1, waiting for transfers between devices, body(): piece = lax.all_gather(joined, 'gx', axis=0, tiled=True)  23.5 us
    psum x1, blocking collectives, body(): lax.psum((jnp.sum(values, axis=1), jnp.sum(values * values, axis=1)), 'gx')  13.8 us
    all_to_all x1, blocking collectives, body(): lax.all_to_all(attended, 'yz', split_axis=1, concat_axis=0, tiled=True)  11.2 us
    dot_general x1, matrix products, body(): jnp.dot(piece[:, query_cols:], down_weight, preferred_element_type=jnp.fl...  8.8 us
    all_to_all x1, starting transfers between devices, body(): lax.all_to_all(fresh_part, 'yz', split_axis=0, concat_axis=2, tiled=True)  6.83 us
  transfers between devices with their start and end apart: 6, of which 6 were waited for; matrix products, arithmetic and copies ran while one was open for 2% of the time, Pallas kernels for 0%

commit v1 on v0

v1 whole, which is shorter than its diff:
```python
import jax
import jax.numpy as jnp
from jax import lax
from jax.sharding import Mesh, PartitionSpec as P

D = 18432
HEADS = 48
HEAD = 256
F32 = jnp.float32
BF16 = jnp.bfloat16
XY = ("x", "y")
ZC = ("z", "c")
ZXY = ("z", "x", "y")
SWAP = [(0, 1), (1, 0)]


def normalize(values, sums, squares, gain):
    mean = sums / D
    var = squares / D - mean * mean
    return ((values - mean[:, None]) * lax.rsqrt(var + 1e-05)[:, None] * gain[None, :]).astype(
        BF16
    )


def attend(query, fresh, cache):
    scale = HEAD ** (-0.5)
    scores = (
        jnp.einsum("rhd,rsd->rhs", query, cache[:, :, :HEAD], preferred_element_type=F32) * scale
    )
    own = jnp.einsum("rhd,rd->rh", query, fresh[:, :HEAD], preferred_element_type=F32) * scale
    highest = jnp.maximum(jnp.max(scores, axis=2), own)
    e_past = jnp.exp(scores - highest[:, :, None])
    e_own = jnp.exp(own - highest)
    total = jnp.sum(e_past, axis=2) + e_own
    w_past = (e_past / total[:, :, None]).astype(BF16)
    w_own = (e_own / total).astype(BF16)
    result = jnp.einsum("rhs,rsd->rhd", w_past, cache[:, :, HEAD:], preferred_element_type=F32)
    result = result + w_own.astype(F32)[:, :, None] * fresh[:, None, HEAD:].astype(F32)
    return result.astype(BF16)


def body(residual, norm_gain, query_weight, kv_weight, cache, ffn_hidden, out_weight, down_weight):
    core = lax.axis_index("c")
    query_cols = query_weight.shape[1]
    fresh_cols = kv_weight.shape[1]
    own_rows, width = residual.shape

    hidden = lax.all_gather(ffn_hidden, ZC, axis=0, tiled=True)

    values = residual.astype(F32)
    sums, squares = lax.psum((jnp.sum(values, axis=1), jnp.sum(values * values, axis=1)), ZC)
    normed = normalize(values, sums, squares, norm_gain)
    gathered = lax.all_to_all(
        jnp.broadcast_to(normed[None], (16, own_rows, width)), XY, 0, 0
    ).reshape(16 * own_rows, width)

    query_term = jnp.dot(gathered, query_weight, preferred_element_type=F32)
    fresh_term = jnp.dot(gathered, kv_weight, preferred_element_type=F32)
    terms = jnp.concatenate([query_term, fresh_term], axis=1).astype(BF16)
    cols = query_cols + fresh_cols
    split = terms.reshape(4, 2, 64, cols)
    mine = lax.dynamic_index_in_dim(split, core, 1, keepdims=False)
    theirs = lax.dynamic_index_in_dim(split, 1 - core, 1, keepdims=False)
    paired = (mine.astype(F32) + lax.ppermute(theirs, "c", SWAP).astype(F32)).astype(BF16)
    parts = lax.all_to_all(paired.reshape(64, 4, cols), ZXY, 0, 0)
    summed = jnp.sum(parts.reshape(4, 16, 4, cols).astype(F32), axis=0).astype(BF16)
    summed = summed.transpose(1, 0, 2)
    query = summed[:, :, :query_cols].reshape(4, HEADS, HEAD)
    fresh = summed[:, :, query_cols:].reshape(4, 2 * HEAD)

    attended = attend(query, fresh, cache).reshape(4, 16, query_cols).transpose(1, 0, 2)
    back = lax.all_to_all(
        jnp.broadcast_to(attended[None], (4, 16, 4, query_cols)).reshape(64, 4, query_cols),
        ZXY, 0, 0,
    ).reshape(4, 1, 64, query_cols)
    other = lax.ppermute(back, "c", SWAP)
    heads = jnp.where(
        core == 0, jnp.concatenate([back, other], axis=1), jnp.concatenate([other, back], axis=1)
    ).reshape(512, query_cols)

    ffn = jnp.dot(hidden, down_weight, preferred_element_type=F32)
    terms = (ffn + jnp.dot(heads, out_weight, preferred_element_type=F32)).astype(BF16)
    pieces = lax.all_to_all(terms.reshape(16, own_rows, width), XY, 0, 0)
    return jnp.sum(pieces.astype(F32), axis=0).astype(BF16)


def solution(mesh):
    fine = Mesh(mesh.devices.reshape(4, 2, 4, 4), ("z", "c", "x", "y"))
    placed = (
        P(XY, ZC),
        P(ZC),
        P(ZC, XY),
        P(ZC, XY),
        P(("z", "c", "x", "y"), None, None),
        P(ZC, XY),
        P(XY, ZC),
        P(XY, ZC),
    )
    return jax.shard_map(body, mesh=fine, in_specs=placed, out_specs=P(XY, ZC), check_vma=False)
```

time: 288 us -> 205 us (0.71)
  waiting for transfers between devices: 190 us -> 34.8 us
  blocking collectives: 25 us -> 90.3 us
  other arithmetic: 10.2 us -> 14.2 us
  starting transfers between devices: 11.1 us -> 7.13 us
  matrix products: 24.6 us -> 28.4 us
    reduce_scatter x2 -> x0, waiting for transfers between devices: 105 us -> none  [the longest x1 74.8 us: body(): lax.psum_scatter(joint_terms.astype(jnp.bfloat16), 'yz', scatter_dimensio...]
    all_gather x2 -> x1, waiting for transfers between devices: 73.9 us -> 0.01 us  [body(): hidden = lax.all_gather(ffn_hidden, ZC, axis=0, tiled=True)]
    all_to_all x1 -> x3, blocking collectives: 11.2 us -> 74.3 us  [the longest x1 34.9 us: body(): pieces = lax.all_to_all(terms.reshape(16, own_rows, width), XY, 0, 0)]
    all_to_all x2 -> x1, waiting for transfers between devices: 10.1 us -> 29.9 us  [body(): lax.all_to_all(jnp.broadcast_to(normed[None], (16, own_rows, width)), XY,...]
    reduce_sum x0 -> x2, other arithmetic: none -> 4.64 us  [the longest x1 2.7 us: body(): return jnp.sum(pieces.astype(F32), axis=0).astype(BF16)]
    ppermute x0 -> x2, waiting for transfers between devices: none -> 4.22 us  [the longest x1 2.16 us: body(): lax.ppermute(theirs, 'c', SWAP).astype(F32)]
    all_to_all x2 -> x1, starting transfers between devices: 11 us -> 7.08 us  [body(): lax.all_to_all(jnp.broadcast_to(normed[None], (16, own_rows, width)), XY,...]
    dot_general x5, matrix products: 17.2 us -> 21 us  [the longest x1 8.86 us: body(): ffn = jnp.dot(hidden, down_weight, preferred_element_type=F32)]
  transfers between devices with their start and end apart: 6 -> 4, of which waited for: 6 -> 3; matrix products, arithmetic and copies ran while one was open for 2% -> 20% of each run, Pallas kernels for 0% -> 0%
where the time goes in v1:
time: 205 us; the launch traced here: 204 us
  blocking collectives  90.3 us (44%)
  waiting for transfers between devices  34.8 us (17%)
  matrix products  28.4 us (14%)
  local copies, waits for them, and re-layouts  15.5 us (8%)
  other arithmetic  14.2 us (7%)
  between operations  13.5 us (7%)
  starting transfers between devices  7.13 us (3%)
    all_to_all x1, blocking collectives, body(): pieces = lax.all_to_all(terms.reshape(16, own_rows, width), XY, 0, 0)  34.9 us
    all_to_all x1, waiting for transfers between devices, body(): lax.all_to_all(jnp.broadcast_to(normed[None], (16, own_rows, width)), XY,...  29.9 us
    all_to_all x1, blocking collectives, body(): parts = lax.all_to_all(paired.reshape(64, 4, cols), ZXY, 0, 0)  23.5 us
    psum x1, blocking collectives, body(): lax.psum((jnp.sum(values, axis=1), jnp.sum(values * values, axis=1)), ZC)  16 us
    all_to_all x1, blocking collectives, body(): lax.all_to_all(jnp.broadcast_to(attended[None], (4, 16, 4, query_cols)).r...  16 us
    dot_general x1, matrix products, body(): ffn = jnp.dot(hidden, down_weight, preferred_element_type=F32)  8.86 us
    all_to_all x1, starting transfers between devices, body(): lax.all_to_all(jnp.broadcast_to(normed[None], (16, own_rows, width)), XY,...  7.08 us
    dot_general x1, matrix products, body(): query_term = jnp.dot(gathered, query_weight, preferred_element_type=F32)  5.63 us
  transfers between devices with their start and end apart: 4, of which 3 were waited for; matrix products, arithmetic and copies ran while one was open for 20% of the time, Pallas kernels for 0%

profile of v1, /device:TPU:0, one launch (start us, length us, event | category | flops | bytes accessed | tf_op | source)
XLA Modules:
  0.0 203.9 jit_solution(15957450853957891458)
XLA Ops:
  6.5 0.0 copy-start
  6.5 1.2 convert_reduce_fusion
  7.7 16.0 %all-reduce = (f32[32]{0:T(128)S(1)}, f32[32]{0:T(128)S(1)}) all-reduce(f32[32]{0:T(128)S(1)} %get-tuple-element.6, f32[32]{0:T(128)S(1)} %get-tuple-element.5), channel_id=1, replica_groups=mesh['z'=4,'c'=2,'x'=4,'y'=4] {'z','c'}, use_global_device_ids=true, to_apply=%region_3.0 | all-reduce | flops 64 | bytes 512 | tf_op jit(solution)/shard_map/psum | solution.py:51
  23.7 1.0 fusion.29
  24.8 1.7 broadcast_in_dim.4
  26.4 7.1 %all-to-all-start = ((bf16[16,32,2304]{2,1,0:T(8,128)(2,1)}), bf16[16,32,2304]{2,1,0:T(8,128)(2,1)}, u32[]{:S(2)}, u32[]{:S(2)}) async-start(bf16[16,32,2304]{2,1,0:T(8,128)(2,1)} %broadcast_in_dim.4), calls=%async_computation | async-start | bytes 4718592 | tf_op jit(solution)/shard_map/all_to_all | solution.py:53
  33.5 0.0 all-gather.2.cloned.1.call-start
  33.6 0.7 all-gather.2.cloned.1.call-update
  34.3 29.9 %all-to-all-done = bf16[16,32,2304]{2,1,0:T(8,128)(2,1)} async-done(((bf16[16,32,2304]{2,1,0:T(8,128)(2,1)}), bf16[16,32,2304]{2,1,0:T(8,128)(2,1)}, u32[]{:S(2)}, u32[]{:S(2)}) %all-to-all-start) | async-done | bytes 2359328 | tf_op jit(solution)/shard_map/all_to_all | solution.py:53
  64.2 0.0 copy-start.2
  64.2 5.6 %fusion.10 = bf16[4,2,64,768]{3,2,1,0:T(8,128)(2,1)} fusion(bf16[4,2,64,2304]{3,2,1,0:T(8,128)(2,1)} %bitcast, bf16[2304,768]{1,0:T(8,128)(2,1)} %param.10), kind=kOutput, calls=%fused_computation.11 | convolution fusion | flops 1812332544 | bytes 6684672 | tf_op jit(solution)/shard_map/dot_general | solution.py:57
  69.8 0.0 copy-done.2
  69.8 3.5 %convolution_convert_fusion = bf16[4,2,64,32]{2,3,1,0:T(8,128)(2,1)} fusion(bf16[4,2,64,2304]{3,2,1,0:T(8,128)(2,1)} %bitcast, bf16[2304,32]{0,1:T(8,128)(2,1)S(1)} %copy-done.2), kind=kOutput, calls=%fused_computation.17 | convolution fusion | flops 75513856 | bytes 2539520 | tf_op jit(solution)/shard_map/dot_general | solution.py:58
  73.3 1.6 copy.18
  74.9 1.8 fusion.24
  76.7 0.0 collective-permute-start
  76.7 2.2 %collective-permute-done = bf16[4,64,800]{2,1,0:T(8,128)(2,1)} collective-permute-done((bf16[4,64,800]{2,1,0:T(8,128)(2,1)}, bf16[4,64,800]{2,1,0:T(8,128)(2,1)}, u32[]{:S(2)}, u32[]{:S(2)}) %collective-permute-start) | collective-permute-done | bytes 409632 | tf_op jit(solution)/shard_map/ppermute | solution.py:64
  78.8 2.0 fusion.20
  80.9 1.9 reshape.49
  82.8 23.5 %all_to_all.20 = bf16[64,4,800]{2,1,0:T(4,128)(2,1)} all-to-all(bf16[64,4,800]{2,1,0:T(4,128)(2,1)} %reshape.49), channel_id=1, replica_groups=mesh['z'=4,'c'=2,'x'=4,'y'=4] {'z','x','y'}, dimensions={0} | all-to-all | bytes 819200 | tf_op jit(solution)/shard_map/all_to_all | solution.py:65
  106.3 1.9 reduce_sum.53
  108.2 1.3 slice.25
  109.5 0.9 slice.24
  110.5 0.7 copy.19
  111.1 1.6 reshape.51
  112.7 0.7 copy.20
  113.4 0.7 reshape.52
  114.1 0.7 slice_convert_fusion
  114.8 1.0 fusion.32
  115.8 3.7 %fusion.36 = (f32[4,48]{1,0:T(4,128)S(1)}, f32[4,48,2048]{2,1,0:T(8,128)S(1)}) fusion(bf16[4,48,256]{2,1,0:T(8,128)(2,1)} %reshape.51, bf16[4,2048,512]{2,1,0:T(8,128)(2,1)} %param.12), kind=kOutput, calls=%fused_computation.48 | convolution fusion | flops 202112832 | bytes 5866240 | tf_op jit(solution)/shard_map/rhd,rsd->rhs/dot_general | solution.py:28
  119.5 0.4 fusion.13
  119.9 3.7 %fusion.17 = bf16[4,48,256]{2,1,0:T(8,128)(2,1)} fusion(bf16[4,2048,512]{2,1,0:T(8,128)(2,1)} %param.12, f32[4,48,2048]{2,1,0:T(8,128)S(1)} %get-tuple-element.16, f32[4,48]{1,0:T(4,128)S(1)} %get-tuple-element.10, f32[4,48]{1,0:T(4,128)S(1)} %multiply_maximum_fusion, f32[4,256]{1,0:T(4,128)S(1)} %get-tuple-element.11, f32[4,48]{1,0:T(4,128)S(1)} %get-tuple-element.9), kind=kOutput, calls=%fused_computation.16 | convolution fusion | flops 202653696 | bytes 5871872 | tf_op jit(solution)/shard_map/rhs,rsd->rhd/dot_general | solution.py:37
  123.6 1.6 reshape.53
  125.2 0.9 copy.21
  126.2 0.1 broadcast_in_dim.5
  126.3 16.0 %all_to_all.21 = bf16[64,4,768]{2,1,0:T(4,128)(2,1)} all-to-all(bf16[64,4,768]{2,1,0:T(4,128)(2,1)S(1)} %bitcast.40), channel_id=1, replica_groups=mesh['z'=4,'c'=2,'x'=4,'y'=4] {'z','x','y'}, dimensions={0} | all-to-all | bytes 786432 | tf_op jit(solution)/shard_map/all_to_all | solution.py:72
  142.2 1.8 reshape.55
  144.1 0.0 collective-permute-start.1
  144.1 2.1 %collective-permute-done.1 = bf16[4,1,64,768]{3,2,1,0:T(8,128)(2,1)} collective-permute-done((bf16[4,1,64,768]{3,2,1,0:T(8,128)(2,1)}, bf16[4,1,64,768]{3,2,1,0:T(8,128)(2,1)}, u32[]{:S(2)}, u32[]{:S(2)}) %collective-permute-start.1) | collective-permute-done | bytes 393248 | tf_op jit(solution)/shard_map/ppermute | solution.py:76
  146.1 2.4 %maximum_select_fusion = bf16[4,2,64,768]{3,2,1,0:T(8,128)(2,1)} fusion(bf16[4,1,64,768]{3,2,1,0:T(8,128)(2,1)} %collective-permute-done.1, bf16[4,1,64,768]{3,2,1,0:T(8,128)(2,1)} %reshape.55, pred[]{:T(512)S(6)} %eq.3), kind=kLoop, calls=%fused_computation.22 | loop fusion | flops 1179648 | bytes 1572865 | tf_op jit(solution)/shard_map/jit(_where)/select_n | solution.py:77
  148.5 0.0 all-gather.2.cloned.1.call-done
  148.5 0.0 copy-start.1
  148.5 8.9 %fusion.37 = f32[512,2304]{1,0:T(8,128)S(1)} fusion(bf16[512,2304]{1,0:T(8,128)(2,1)} %all-gather.2.cloned.1.call-done, bf16[2304,2304]{1,0:T(8,128)(2,1)} %param.15), kind=kOutput, calls=%fused_computation.49 | convolution fusion | flops 5435817984 | bytes 17694720 | tf_op jit(solution)/shard_map/dot_general | solution.py:81
  157.4 0.0 copy-done
  157.4 0.0 copy-done.1
  157.4 2.0 %fusion = bf16[512,2304]{1,0:T(8,128)(2,1)S(1)} fusion(f32[512,2304]{1,0:T(8,128)S(1)} %fusion.37, bf16[512,768]{1,0:T(8,128)(2,1)S(1)} %bitcast.41, bf16[768,2304]{1,0:T(8,128)(2,1)S(1)} %copy-done), kind=kOutput, calls=%fused_computation.1 | convolution fusion | flops 1814298624 | bytes 11403264 | tf_op jit(solution)/shard_map/dot_general | solution.py:82
  159.5 34.9 %all_to_all.22 = bf16[16,32,2304]{2,1,0:T(8,128)(2,1)} all-to-all(bf16[16,32,2304]{2,1,0:T(8,128)(2,1)S(1)} %bitcast.38), channel_id=1, replica_groups=mesh['z'=4,'c'=2,'x'=4,'y'=4] {'x','y'}, dimensions={0} | all-to-all | bytes 4718592 | tf_op jit(solution)/shard_map/all_to_all | solution.py:83
  194.3 2.7 %reduce_sum.55 = bf16[32,2304]{1,0:T(8,128)(2,1)} reduce(bf16[16,32,2304]{2,1,0:T(8,128)(2,1)} %all_to_all.22, bf16[]{:T(256)} %constant.32.clone.1), dimensions={0}, to_apply=%region_7.8 | reduce | flops 1105920 | bytes 2506754 | tf_op jit(solution)/shard_map/reduce_sum | solution.py:84
  (3 shorter events, 0.0 us)
Async XLA Ops:
  6.5 150.9 %copy-start = (bf16[768,2304]{1,0:T(8,128)(2,1)S(1)}, bf16[768,2304]{1,0:T(8,128)(2,1)}, u32[]{:S(2)}) copy-start(bf16[768,2304]{1,0:T(8,128)(2,1)} %param.14) | copy-start | bytes 10616836
  26.4 37.7 %all-to-all-start = ((bf16[16,32,2304]{2,1,0:T(8,128)(2,1)}), bf16[16,32,2304]{2,1,0:T(8,128)(2,1)}, u32[]{:S(2)}, u32[]{:S(2)}) async-start(bf16[16,32,2304]{2,1,0:T(8,128)(2,1)} %broadcast_in_dim.4), calls=%async_computation | async-start | bytes 4718592 | tf_op jit(solution)/shard_map/all_to_all | solution.py:53
  33.5 115.0 %all-gather.2.cloned.1.call-start = ((), (), s32[]{:S(2)}) async-start(), calls=%async_computation.4 | async-start | bytes 2654208 | tf_op jit(solution)/shard_map/all_gather | solution.py:48
  64.2 5.6 %copy-start.2 = (bf16[2304,32]{0,1:T(8,128)(2,1)S(1)}, bf16[2304,32]{0,1:T(8,128)(2,1)}, u32[]{:S(2)}) copy-start(bf16[2304,32]{0,1:T(8,128)(2,1)} %param.11) | copy-start | bytes 442372
  76.7 2.2 %collective-permute-start = (bf16[4,64,800]{2,1,0:T(8,128)(2,1)}, bf16[4,64,800]{2,1,0:T(8,128)(2,1)}, u32[]{:S(2)}, u32[]{:S(2)}) collective-permute-start(bf16[4,64,800]{2,1,0:T(8,128)(2,1)} %fusion.24), channel_id=1, source_target_pairs={{0,16},{16,0},{1,17},{17,1},{2,18},{18,2},{3,19},{19,3},{4,20},{20... | collective-permute-start | bytes 1228808 | tf_op jit(solution)/shard_map/ppermute | solution.py:64
  144.1 2.1 %collective-permute-start.1 = (bf16[4,1,64,768]{3,2,1,0:T(8,128)(2,1)}, bf16[4,1,64,768]{3,2,1,0:T(8,128)(2,1)}, u32[]{:S(2)}, u32[]{:S(2)}) collective-permute-start(bf16[4,1,64,768]{3,2,1,0:T(8,128)(2,1)} %reshape.55), channel_id=1, source_target_pairs={{0,16},{16,0},{1,17},{17,1},{2,18},{18,2},{3,19},{19,3},{4,20},{20... | collective-permute-start | bytes 1179656 | tf_op jit(solution)/shard_map/ppermute | solution.py:76
  148.5 8.9 %copy-start.1 = (bf16[4,2,64,768]{3,2,1,0:T(8,128)(2,1)S(1)}, bf16[4,2,64,768]{3,2,1,0:T(8,128)(2,1)}, u32[]{:S(2)}) copy-start(bf16[4,2,64,768]{3,2,1,0:T(8,128)(2,1)} %maximum_select_fusion) | copy-start | bytes 2359300
Sparse Core Ops, SparseCore 0:
  36.0 24.8 all-gather.1

commit v2 on v1

v2 whole, which is shorter than its diff:
```python
import functools

import jax
import jax.numpy as jnp
from jax import lax
from jax.experimental import pallas as pl
from jax.experimental.pallas import tpu as pltpu
from jax.sharding import Mesh, PartitionSpec as P

D = 18432
HEADS = 48
HEAD = 256
F32 = jnp.float32
BF16 = jnp.bfloat16
XY = ("x", "y")
ZC = ("z", "c")
ZXY = ("z", "x", "y")
SWAP = [(0, 1), (1, 0)]
WIDE = 58 << 20
NARROW = 8 << 20


def lower_rows(shape):
    return lax.broadcasted_iota(jnp.int32, shape, 1) < 4


def moments_kernel(residual_ref, out_ref):
    values = residual_ref[...].astype(F32)
    sums = jnp.sum(values, axis=1, keepdims=True)
    squares = jnp.sum(values * values, axis=1, keepdims=True)
    lanes = lax.broadcasted_iota(jnp.int32, out_ref.shape, 1)
    out_ref[...] = jnp.where(lanes < 64, sums, squares)


def row_moments(residual):
    return pl.pallas_call(
        moments_kernel,
        out_shape=jax.ShapeDtypeStruct((residual.shape[0], 128), F32),
        compiler_params=pltpu.CompilerParams(vmem_limit_bytes=NARROW),
        name="row_moments",
    )(residual)


def normalize_kernel(residual_ref, moments_ref, more_ref, gain_ref, out_ref):
    moments = moments_ref[...] + more_ref[...]
    mean = moments[:, 0:1] / D
    var = moments[:, 64:65] / D - mean * mean
    values = residual_ref[...].astype(F32)
    normed = ((values - mean) * lax.rsqrt(var + 1e-05) * gain_ref[...]).astype(BF16)
    for i in range(out_ref.shape[0]):
        out_ref[i] = normed


def normalize(residual, moments, more, gain):
    rows, width = residual.shape
    return pl.pallas_call(
        normalize_kernel,
        out_shape=jax.ShapeDtypeStruct((16, rows, width), BF16),
        compiler_params=pltpu.CompilerParams(vmem_limit_bytes=NARROW),
        name="normalize",
    )(residual, moments, more, gain)


def feed_kernel(own_ref, other_ref, weight_ref, out_ref):
    rows = own_ref.shape[0]
    weight = weight_ref[...]
    out_ref[:rows, :] = jnp.dot(own_ref[...], weight, preferred_element_type=F32)
    out_ref[rows:, :] = jnp.dot(other_ref[...], weight, preferred_element_type=F32)


def feed(own, other, weight):
    rows, depth = own.shape
    width = weight.shape[1]
    tile = 256
    whole = pl.BlockSpec((rows, depth), lambda i: (0, 0), pipeline_mode=pl.Buffered(1))
    return pl.pallas_call(
        feed_kernel,
        grid=(width // tile,),
        in_specs=[whole, whole, pl.BlockSpec((depth, tile), lambda i: (0, i))],
        out_specs=pl.BlockSpec((2 * rows, tile), lambda i: (0, i)),
        out_shape=jax.ShapeDtypeStruct((2 * rows, width), F32),
        compiler_params=pltpu.CompilerParams(vmem_limit_bytes=WIDE),
        cost_estimate=pl.CostEstimate(flops=1, bytes_accessed=1, transcendentals=0),
        name="feed",
    )(own, other, weight)


def project_kernel(x_ref, query_ref, fresh_ref, mine_ref, theirs_ref, slots_ref):
    core = lax.axis_index("c")
    step = pl.program_id(0)

    @pl.when(step < 3)
    def _():
        slots_ref[step] = jnp.dot(x_ref[...], query_ref[...], preferred_element_type=F32)

    @pl.when(step == 3)
    def _():
        fresh = jnp.dot(x_ref[...], fresh_ref[...], preferred_element_type=F32)
        fresh = jnp.concatenate([fresh, jnp.zeros_like(fresh)], axis=1)
        low = lower_rows((8, 8, HEAD))
        for block in range(8):
            z, c = block // 2, block % 2
            rows = slice(block * 64, block * 64 + 64)
            s = [slots_ref[h, rows, :] for h in range(3)] + [fresh[rows]]
            s = [v.reshape(8, 8, HEAD) for v in s]
            r = [pltpu.roll(v, 4, 1) for v in s]
            even = jnp.concatenate([jnp.where(low, s[0], r[1]), jnp.where(low, s[2], r[3])], axis=1)
            odd = jnp.concatenate([jnp.where(low, r[0], s[1]), jnp.where(low, r[2], s[3])], axis=1)

            def put(ref, z=z, even=even, odd=odd):
                ref[z, :, 0] = even.astype(BF16)
                ref[z, :, 1] = odd.astype(BF16)

            pl.when(core == c)(functools.partial(put, mine_ref))
            pl.when(core != c)(functools.partial(put, theirs_ref))


def project(x, query_weight, fresh_weight):
    rows, width = x.shape
    out = jax.ShapeDtypeStruct((4, 8, 2, 16, HEAD), BF16)
    return pl.pallas_call(
        project_kernel,
        grid=(4,),
        in_specs=[
            pl.BlockSpec((rows, width), lambda i: (0, 0), pipeline_mode=pl.Buffered(1)),
            pl.BlockSpec((width, HEAD), lambda i: (0, jnp.minimum(i, 2))),
            pl.BlockSpec(fresh_weight.shape, lambda i: (0, 0), pipeline_mode=pl.Buffered(1)),
        ],
        out_specs=[pl.BlockSpec(out.shape, lambda i: (0, 0, 0, 0, 0))] * 2,
        out_shape=[out, out],
        scratch_shapes=[pltpu.VMEM((3, rows, HEAD), F32)],
        compiler_params=pltpu.CompilerParams(vmem_limit_bytes=48 << 20),
        cost_estimate=pl.CostEstimate(
            flops=2 * rows * width * 896, bytes_accessed=8 << 20, transcendentals=0
        ),
        name="project",
    )(x, query_weight, fresh_weight)


def attend_kernel(parts_ref, cache_ref, out_ref, held_ref, sums_ref, result_ref, sems):
    copies = [
        pltpu.make_async_copy(cache_ref.at[t], held_ref.at[t], sems.at[t]) for t in range(4)
    ]
    for copy in copies:
        copy.start()
    total = parts_ref[0].astype(F32)
    for z in range(1, 4):
        total = total + parts_ref[z].astype(F32)
    total = total.astype(BF16).astype(F32).reshape(256, HEAD)
    for half in range(2):
        sums_ref[half] = total[:, half * 128 : half * 128 + 128]
        result_ref[half] = jnp.zeros((256, 128), F32)
    scale = HEAD ** (-0.5)
    for t in range(4):

        def slot(h):
            return jnp.concatenate(
                [sums_ref[half, pl.ds(h * 4 + t, 16, stride=16), :] for half in range(2)], axis=1
            )

        query = jnp.concatenate([slot(h) for h in range(3)], axis=0)
        columns = sums_ref[0, pl.ds(12 + t, 16, stride=16), :]
        fresh = [jnp.sum(columns[4 * b : 4 * b + 4], axis=0, keepdims=True) for b in range(4)]
        new_key = jnp.concatenate(fresh[:2], axis=1)
        new_value = jnp.concatenate(fresh[2:], axis=1)
        own = jnp.sum(query * new_key, axis=1, keepdims=True) * scale
        copies[t].wait()
        scores = (
            lax.dot_general(
                query.astype(BF16),
                held_ref[t, :, :HEAD],
                (((1,), (1,)), ((), ())),
                preferred_element_type=F32,
            )
            * scale
        )
        highest = jnp.maximum(jnp.max(scores, axis=1, keepdims=True), own)
        e_past = jnp.exp(scores - highest)
        e_own = jnp.exp(own - highest)
        total = jnp.sum(e_past, axis=1, keepdims=True) + e_own
        result = jnp.dot(e_past.astype(BF16), held_ref[t, :, HEAD:], preferred_element_type=F32)
        result = (result + e_own * new_value) / total
        for h in range(3):
            for half in range(2):
                result_ref[half, pl.ds(h * 4 + t, 16, stride=16), :] = result[
                    h * 16 : h * 16 + 16, half * 128 : half * 128 + 128
                ]
    whole = jnp.concatenate([result_ref[0], result_ref[1]], axis=1)
    whole = whole.reshape(16, 16, HEAD).astype(BF16)
    for z in range(4):
        out_ref[z] = whole


def attend(parts, cache):
    return pl.pallas_call(
        attend_kernel,
        in_specs=[
            pl.BlockSpec(memory_space=pltpu.VMEM),
            pl.BlockSpec(memory_space=pl.ANY),
        ],
        out_specs=pl.BlockSpec(memory_space=pltpu.VMEM),
        out_shape=jax.ShapeDtypeStruct((4, 16, 16, HEAD), BF16),
        scratch_shapes=[
            pltpu.VMEM(cache.shape, BF16),
            pltpu.VMEM((2, 256, 128), F32),
            pltpu.VMEM((2, 256, 128), F32),
            pltpu.SemaphoreType.DMA((4,)),
        ],
        compiler_params=pltpu.CompilerParams(vmem_limit_bytes=WIDE),
        cost_estimate=pl.CostEstimate(
            flops=4 * 4 * 48 * 2048 * 256, bytes_accessed=10 << 20, transcendentals=1 << 19
        ),
        name="attend",
    )(parts, cache)


def output_kernel(back_ref, other_ref, weight_ref, ffn_ref, out_ref, heads_ref):
    core = lax.axis_index("c")
    z_here = lax.axis_index("z")
    tile = out_ref.shape[1]

    @pl.when(pl.program_id(0) == 0)
    def _():
        low = lower_rows((8, 8, HEAD))
        for rel, ref in ((0, back_ref), (1, other_ref)):
            for z in range(4):
                even = ref[z, :, 0].astype(F32)
                odd = ref[z, :, 1].astype(F32)
                e0, e1, o0, o1 = even[:, :8], even[:, 8:], odd[:, :8], odd[:, 8:]
                heads = [
                    jnp.where(low, e0, pltpu.roll(o0, 4, 1)),
                    jnp.where(low, pltpu.roll(e0, 4, 1), o0),
                    jnp.where(low, e1, pltpu.roll(o1, 4, 1)),
                ]
                c = core if rel == 0 else 1 - core
                rows = pl.ds(pl.multiple_of(z * 128 + c * 64, 64), 64)
                for h in range(3):
                    heads_ref[rows, h * HEAD : (h + 1) * HEAD] = heads[h].reshape(64, HEAD).astype(BF16)

    terms = jnp.dot(heads_ref[...], weight_ref[...], preferred_element_type=F32)
    for z in range(4):
        away = (z_here - z + 4) % 4
        slot = jnp.where(away == 0, 0, jnp.where(away == 1, 1, jnp.where(away == 3, 2, 3)))
        for c in range(2):
            rel = jnp.where(core == c, 0, 4)
            here = pl.ds(pl.multiple_of((rel + slot) * 64, 64), 64)
            row = z * 128 + c * 64
            out_ref[row : row + 64, :] = (terms[row : row + 64] + ffn_ref[here, :]).astype(BF16)


def output(back, other, weight, ffn):
    rows, width = ffn.shape
    tile = 768
    whole = pl.BlockSpec((4, 8, 2, 16, HEAD), lambda i: (0, 0, 0, 0, 0), pipeline_mode=pl.Buffered(1))
    return pl.pallas_call(
        output_kernel,
        grid=(width // tile,),
        in_specs=[
            whole,
            whole,
            pl.BlockSpec((weight.shape[0], tile), lambda i: (0, i)),
            pl.BlockSpec((rows, tile), lambda i: (0, i)),
        ],
        out_specs=pl.BlockSpec((rows, tile), lambda i: (0, i)),
        out_shape=jax.ShapeDtypeStruct((rows, width), BF16),
        scratch_shapes=[pltpu.VMEM((rows, weight.shape[0]), BF16)],
        compiler_params=pltpu.CompilerParams(vmem_limit_bytes=20 << 20),
        cost_estimate=pl.CostEstimate(flops=2 * rows * width * 768, bytes_accessed=12 << 20, transcendentals=0),
        name="output",
    )(back, other, weight, ffn)


def add_kernel(pieces_ref, out_ref):
    total = pieces_ref[0].astype(F32)
    for i in range(1, pieces_ref.shape[0]):
        total = total + pieces_ref[i].astype(F32)
    out_ref[...] = total.astype(BF16)


def add_pieces(pieces):
    count, rows, width = pieces.shape
    tile = 768
    return pl.pallas_call(
        add_kernel,
        grid=(width // tile,),
        in_specs=[pl.BlockSpec((count, rows, tile), lambda i: (0, 0, i))],
        out_specs=pl.BlockSpec((rows, tile), lambda i: (0, i)),
        out_shape=jax.ShapeDtypeStruct((rows, width), BF16),
        compiler_params=pltpu.CompilerParams(vmem_limit_bytes=NARROW),
        name="add_pieces",
    )(pieces)


def body(residual, norm_gain, query_weight, kv_weight, cache, ffn_hidden, out_weight, down_weight):
    own_rows, width = residual.shape
    place = lax.axis_index(XY)
    rows = 16 * own_rows

    moments = row_moments(residual)
    moments = moments + lax.ppermute(moments, "c", SWAP)
    moments = moments + lax.ppermute(moments, "z", [(i, i ^ 1) for i in range(4)])
    more = lax.ppermute(moments, "z", [(i, i ^ 2) for i in range(4)])
    copies = normalize(residual, moments, more, norm_gain[None, :])
    copies, ffn_hidden, kv_weight = lax.optimization_barrier((copies, ffn_hidden, kv_weight))
    normed = lax.all_to_all(copies, XY, 0, 0).reshape(rows, width)

    hidden = jnp.concatenate(
        [ffn_hidden]
        + [lax.ppermute(ffn_hidden, "z", [(i, (i + k) % 4) for i in range(4)]) for k in (1, 3, 2)]
    )
    ffn = feed(hidden, lax.ppermute(hidden, "c", SWAP), down_weight)
    columns = kv_weight.shape[1]
    mask = jnp.arange(128)[None, :] // columns == place % 4
    fresh_weight = jnp.where(mask, jnp.tile(kv_weight, (1, 128 // columns)), 0)
    normed, fresh_weight, ffn = lax.optimization_barrier((normed, fresh_weight, ffn))

    mine, theirs = project(normed, query_weight, fresh_weight)
    paired = (mine.astype(F32) + lax.ppermute(theirs, "c", SWAP).astype(F32)).astype(BF16)
    parts = lax.all_to_all(paired.reshape(64, 16, HEAD), ZXY, 0, 0)

    attended = attend(parts.reshape(4, 16, 16, HEAD), cache)
    back = lax.all_to_all(attended.reshape(64, 16, HEAD), ZXY, 0, 0).reshape(4, 8, 2, 16, HEAD)
    other = lax.ppermute(back, "c", SWAP)
    terms = output(back, other, out_weight, ffn)
    pieces = lax.all_to_all(terms.reshape(16, own_rows, width), XY, 0, 0)
    return add_pieces(pieces)


def solution(mesh):
    fine = Mesh(mesh.devices.reshape(4, 2, 4, 4), ("z", "c", "x", "y"))
    placed = (
        P(XY, ZC),
        P(ZC),
        P(ZC, XY),
        P(ZC, XY),
        P(("z", "c", "x", "y"), None, None),
        P(ZC, XY),
        P(XY, ZC),
        P(XY, ZC),
    )
    return jax.shard_map(body, mesh=fine, in_specs=placed, out_specs=P(XY, ZC), check_vma=False)
```

time: 205 us -> 154 us (0.75)
  Pallas kernels: 0 us -> 32.7 us
  matrix products: 28.4 us -> 0 us
  blocking collectives: 90.3 us -> 71.7 us
  other arithmetic: 14.2 us -> 0.24 us
  between operations: 13.5 us -> 0.11 us
  waiting for transfers between devices: 34.8 us -> 21.9 us
  starting transfers between devices: 7.13 us -> 18.7 us
  local copies, waits for them, and re-layouts: 15.5 us -> 7.9 us
    pallas_call x0 -> x7, Pallas kernels: none -> 32.7 us  [the longest x1 12.7 us: feed(): pl.pallas_call(feed_kernel, grid=(width // tile,), in_specs=[whole, whole...]
    dot_general x7 -> x0, matrix products: 28.4 us -> none  [the longest x1 8.86 us: body(): ffn = jnp.dot(hidden, down_weight, preferred_element_type=F32)]
    all_to_all x1, waiting for transfers between devices: 29.9 us -> 9.84 us  [body(): normed = lax.all_to_all(copies, XY, 0, 0).reshape(rows, width)]
    psum x1 -> x0, blocking collectives: 16 us -> none  [body(): lax.psum((jnp.sum(values, axis=1), jnp.sum(values * values, axis=1)), ZC)]
    ppermute x0 -> x7, starting transfers between devices: none -> 11.6 us  [the longest x3 5.55 us: body(): lax.ppermute(ffn_hidden, 'z', [(i, (i + k) % 4) for i in range(4)])]
    ppermute x0 -> x7, waiting for transfers between devices: none -> 8.23 us  [the longest x1 2.76 us: body(): ffn = feed(hidden, lax.ppermute(hidden, 'c', SWAP), down_weight)]
    reshape x5 -> x0, local copies, waits for them, and re-layouts: 7.58 us -> none  [the longest x1 1.91 us: body(): parts = lax.all_to_all(paired.reshape(64, 4, cols), ZXY, 0, 0)]
    reduce_sum x4 -> x0, other arithmetic: 6.22 us -> none  [the longest x1 2.7 us: body(): return jnp.sum(pieces.astype(F32), axis=0).astype(BF16)]
  transfers between devices with their start and end apart: 4 -> 10, of which waited for: 3 -> 8; matrix products, arithmetic and copies ran while one was open for 20% -> 3% of each run, Pallas kernels for 0% -> 8%
where the time goes in v2:
time: 154 us; the launch traced here: 153 us
  blocking collectives  71.7 us (47%)
  Pallas kernels  32.7 us (21%)
  waiting for transfers between devices  21.9 us (14%)
  starting transfers between devices  18.7 us (12%)
  local copies, waits for them, and re-layouts  7.9 us (5%)
    all_to_all x1, blocking collectives, body(): pieces = lax.all_to_all(terms.reshape(16, own_rows, width), XY, 0, 0)  34.3 us
    all_to_all x1, blocking collectives, body(): parts = lax.all_to_all(paired.reshape(64, 16, HEAD), ZXY, 0, 0)  20.5 us
    all_to_all x1, blocking collectives, body(): lax.all_to_all(attended.reshape(64, 16, HEAD), ZXY, 0, 0)  16.9 us
    pallas_call x1, Pallas kernels, feed(): pl.pallas_call(feed_kernel, grid=(width // tile,), in_specs=[whole, whole...  12.7 us
    all_to_all x1, waiting for transfers between devices, body(): normed = lax.all_to_all(copies, XY, 0, 0).reshape(rows, width)  9.84 us
    pallas_call x1, Pallas kernels, attend(): pl.pallas_call(attend_kernel, in_specs=[pl.BlockSpec(memory_space=pltpu.V...  8.11 us
    all_to_all x1, starting transfers between devices, body(): normed = lax.all_to_all(copies, XY, 0, 0).reshape(rows, width)  7.03 us
    unnamed x17, local copies, waits for them, and re-layouts  6.11 us
  transfers between devices with their start and end apart: 10, of which 8 were waited for; matrix products, arithmetic and copies ran while one was open for 3% of the time, Pallas kernels for 8%

profile of v2, /device:TPU:0, one launch (start us, length us, event | category | flops | bytes accessed | tf_op | source)
XLA Modules:
  0.0 153.2 jit_solution(8980755122520801296)
XLA Ops:
  0.0 0.0 copy-start.1
  0.0 0.9 copy-done.1
  0.9 0.1 row_moments.1
  1.0 0.1 collective-permute-start
  1.1 1.2 collective-permute-done
  2.3 2.0 %collective-permute-start.1 = (f32[32,128]{1,0:T(8,128)S(1)}, f32[32,128]{1,0:T(8,128)S(1)}, u32[]{:S(2)}, u32[]{:S(2)}) collective-permute-start(f32[32,128]{1,0:T(8,128)S(1)} %add.22), channel_id=1, source_target_pairs={{0,32},{32,0},{64,96},{96,64},{1,33},{33,1},{65,97},{97,65},{2,34}... | collective-permute-start | bytes 49160 | tf_op jit(solution)/shard_map/ppermute | solution.py:301
  4.3 1.7 %collective-permute-done.1 = f32[32,128]{1,0:T(8,128)S(1)} collective-permute-done((f32[32,128]{1,0:T(8,128)S(1)}, f32[32,128]{1,0:T(8,128)S(1)}, u32[]{:S(2)}, u32[]{:S(2)}) %collective-permute-start.1) | collective-permute-done | bytes 16416 | tf_op jit(solution)/shard_map/ppermute | solution.py:301
  6.0 4.0 %collective-permute-start.2 = (f32[32,128]{1,0:T(8,128)S(1)}, f32[32,128]{1,0:T(8,128)S(1)}, u32[]{:S(2)}, u32[]{:S(2)}) collective-permute-start(f32[32,128]{1,0:T(8,128)S(1)} %add.23.moments_ref), channel_id=1, source_target_pairs={{0,64},{32,96},{64,0},{96,32},{1,65},{33,97},{65,1},{97,33},{2,66}... | collective-permute-start | bytes 49160 | tf_op jit(solution)/shard_map/ppermute | solution.py:302
  10.0 0.7 broadcast_in_dim.16.gain_ref
  10.7 1.0 collective-permute-done.2.more_ref
  11.7 0.0 copy-start.2
  11.7 0.9 copy-done.2
  12.6 0.0 copy-start.3
  12.6 1.8 %normalize.1 = bf16[16,32,2304]{2,1,0:T(8,128)(2,1)} custom-call(bf16[32,2304]{1,0:T(8,128)(2,1)S(1)} %copy-done.2, f32[32,128]{1,0:T(8,128)S(1)} %add.23.moments_ref, f32[32,128]{1,0:T(8,128)S(1)} %collective-permute-done.2.more_ref, f32[1,2304]{1,0:T(1,128)S(1)} %broadcast_in_dim.16.gain_ref), custom_call_target="tpu_custom_call" | custom-call | tf_op jit(solution)/shard_map/normalize/pallas_call | solution.py:56
  14.4 0.0 copy-done.3
  14.4 3.5 %collective-permute-start.5 = (bf16[64,2304]{1,0:T(8,128)(2,1)S(1)}, bf16[64,2304]{1,0:T(8,128)(2,1)S(1)}, u32[]{:S(2)}, u32[]{:S(2)}) collective-permute-start(bf16[64,2304]{1,0:T(8,128)(2,1)S(1)} %copy-done.3), channel_id=1, source_target_pairs={{0,64},{32,96},{64,0},{96,32},{1,65},{33,97},{65,1},{97,33},{2,66}... | collective-permute-start | bytes 884744 | tf_op jit(solution)/shard_map/ppermute | solution.py:309
  17.9 0.7 collective-permute-start.4
  18.6 1.3 collective-permute-start.3
  19.9 7.0 %all-to-all-start = ((bf16[16,32,2304]{2,1,0:T(8,128)(2,1)}), bf16[16,32,2304]{2,1,0:T(8,128)(2,1)S(1)}, u32[]{:S(2)}, u32[]{:S(2)}) async-start(bf16[16,32,2304]{2,1,0:T(8,128)(2,1)} %normalize.1), calls=%async_computation | async-start | bytes 4718592 | tf_op jit(solution)/shard_map/all_to_all | solution.py:305
  27.0 0.8 constant_dynamic-update-slice_fusion.3
  27.7 1.5 %collective-permute-done.3 = bf16[64,2304]{1,0:T(8,128)(2,1)S(1)} collective-permute-done((bf16[64,2304]{1,0:T(8,128)(2,1)S(1)}, bf16[64,2304]{1,0:T(8,128)(2,1)S(1)}, u32[]{:S(2)}, u32[]{:S(2)}) %collective-permute-start.3) | collective-permute-done | bytes 294944 | tf_op jit(solution)/shard_map/ppermute | solution.py:309
  29.2 0.8 constant_dynamic-update-slice_fusion.2
  30.0 0.0 copy-start.4
  30.0 0.0 collective-permute-done.4
  30.0 0.8 constant_dynamic-update-slice_fusion.1
  30.8 0.0 collective-permute-done.5
  30.8 0.7 constant_dynamic-update-slice_fusion.own_ref
  31.5 0.0 collective-permute-start.6
  31.5 0.0 copy-done.4
  31.6 0.3 copy.10
  31.9 2.8 %collective-permute-done.6.other_ref = bf16[256,2304]{1,0:T(8,128)(2,1)} collective-permute-done((bf16[256,2304]{1,0:T(8,128)(2,1)}, bf16[256,2304]{1,0:T(8,128)(2,1)}, u32[]{:S(2)}, u32[]{:S(2)}) %collective-permute-start.6) | collective-permute-done | bytes 1179680 | tf_op jit(solution)/shard_map/ppermute | solution.py:311
  34.7 12.7 %feed.1.ffn_ref = f32[512,2304]{1,0:T(8,128)} custom-call(bf16[256,2304]{1,0:T(8,128)(2,1)} %constant_dynamic-update-slice_fusion.own_ref, bf16[256,2304]{1,0:T(8,128)(2,1)} %collective-permute-done.6.other_ref, bf16[2304,2304]{1,0:T(8,128)(2,1)} %weight_ref.2), custom_call_target="tpu_custom_call" | custom-call | flops 1 | bytes 1 | tf_op jit(solution)/shard_map/feed/pallas_call | solution.py:76
  47.4 9.8 %all-to-all-done = bf16[16,32,2304]{2,1,0:T(8,128)(2,1)S(1)} async-done(((bf16[16,32,2304]{2,1,0:T(8,128)(2,1)}), bf16[16,32,2304]{2,1,0:T(8,128)(2,1)S(1)}, u32[]{:S(2)}, u32[]{:S(2)}) %all-to-all-start) | async-done | bytes 2359328 | tf_op jit(solution)/shard_map/all_to_all | solution.py:305
  57.3 5.2 %project.1 = (bf16[4,8,2,16,256]{4,3,2,1,0:T(8,128)(2,1)S(1)}, bf16[4,8,2,16,256]{4,3,2,1,0:T(8,128)(2,1)S(1)}) custom-call(bf16[512,2304]{1,0:T(8,128)(2,1)S(1)} %bitcast.10, bf16[2304,768]{1,0:T(8,128)(2,1)} %query_ref.1, bf16[2304,128]{1,0:T(8,128)(2,1)S(1)} %broadcast_select_fusion.fresh_ref), custom_call_target="tpu_custom_call" | custom-call | flops 2113929216 | bytes 8388608 | tf_op jit(solution)/shard_map/project/pallas_call | solution.py:121
  62.5 0.1 collective-permute-start.7
  62.6 1.9 %collective-permute-done.7 = bf16[4,8,2,16,256]{4,3,2,1,0:T(8,128)(2,1)S(1)} collective-permute-done((bf16[4,8,2,16,256]{4,3,2,1,0:T(8,128)(2,1)S(1)}, bf16[4,8,2,16,256]{4,3,2,1,0:T(8,128)(2,1)S(1)}, u32[]{:S(2)}, u32[]{:S(2)}) %collective-permute-start.7) | collective-permute-done | bytes 524320 | tf_op jit(solution)/shard_map/ppermute | solution.py:318
  64.5 0.2 add_convert_fusion
  64.6 20.5 %all_to_all.20 = bf16[64,16,256]{2,1,0:T(8,128)(2,1)} all-to-all(bf16[64,16,256]{2,1,0:T(8,128)(2,1)S(1)} %bitcast.14), channel_id=1, replica_groups=mesh['z'=4,'c'=2,'x'=4,'y'=4] {'z','x','y'}, dimensions={0} | all-to-all | bytes 1048576 | tf_op jit(solution)/shard_map/all_to_all | solution.py:319
  85.1 8.1 %attend.1 = bf16[4,16,16,256]{3,2,1,0:T(8,128)(2,1)} custom-call(bf16[4,16,16,256]{3,2,1,0:T(8,128)(2,1)} %bitcast.15, bf16[4,2048,512]{2,1,0:T(8,128)(2,1)} %cache_ref.1), custom_call_target="tpu_custom_call" | custom-call | flops 402653184 | bytes 10485760 | tf_op jit(solution)/shard_map/attend/pallas_call | solution.py:195
  93.2 16.9 %all_to_all.21 = bf16[64,16,256]{2,1,0:T(8,128)(2,1)S(1)} all-to-all(bf16[64,16,256]{2,1,0:T(8,128)(2,1)} %bitcast.16), channel_id=1, replica_groups=mesh['z'=4,'c'=2,'x'=4,'y'=4] {'z','x','y'}, dimensions={0} | all-to-all | bytes 1048576 | tf_op jit(solution)/shard_map/all_to_all | solution.py:322
  110.2 0.0 collective-permute-start.8
  110.2 1.9 %collective-permute-done.8.other_ref = bf16[4,8,2,16,256]{4,3,2,1,0:T(8,128)(2,1)S(1)} collective-permute-done((bf16[4,8,2,16,256]{4,3,2,1,0:T(8,128)(2,1)S(1)}, bf16[4,8,2,16,256]{4,3,2,1,0:T(8,128)(2,1)S(1)}, u32[]{:S(2)}, u32[]{:S(2)}) %collective-permute-start.8) | collective-permute-done | bytes 524320 | tf_op jit(solution)/shard_map/ppermute | solution.py:323
  112.1 0.0 slice-done
  112.1 0.0 slice-done.1
  112.1 2.0 %copy-done = bf16[768,2304]{1,0:T(8,128)(2,1)S(1)} copy-done((bf16[768,2304]{1,0:T(8,128)(2,1)S(1)}, bf16[768,2304]{1,0:T(8,128)(2,1)}, u32[]{:S(2)}) %copy-start) | copy-done | bytes 3538968
  114.1 3.3 %output.1 = bf16[512,2304]{1,0:T(8,128)(2,1)S(1)} custom-call(bf16[4,8,2,16,256]{4,3,2,1,0:T(8,128)(2,1)S(1)} %bitcast.12, bf16[4,8,2,16,256]{4,3,2,1,0:T(8,128)(2,1)S(1)} %collective-permute-done.8.other_ref, bf16[768,2304]{1,0:T(8,128)(2,1)S(1)} %copy-done, f32[512,2304]{1,0:T(8,128)S(1)} %bitcast.8), custom_call_target="tpu_custom_call" | custom-call | flops 1811939328 | bytes 12582912 | tf_op jit(solution)/shard_map/output/pallas_call | solution.py:255
  117.4 34.3 %all_to_all.22.pieces_ref = bf16[16,32,2304]{2,1,0:T(8,128)(2,1)S(1)} all-to-all(bf16[16,32,2304]{2,1,0:T(8,128)(2,1)S(1)} %bitcast.9), channel_id=1, replica_groups=mesh['z'=4,'c'=2,'x'=4,'y'=4] {'x','y'}, dimensions={0} | all-to-all | bytes 4718592 | tf_op jit(solution)/shard_map/all_to_all | solution.py:325
  151.7 1.6 %add_pieces.1 = bf16[32,2304]{1,0:T(8,128)(2,1)} custom-call(bf16[16,32,2304]{2,1,0:T(8,128)(2,1)S(1)} %all_to_all.22.pieces_ref), custom_call_target="tpu_custom_call" | custom-call | tf_op jit(solution)/shard_map/add_pieces/pallas_call | solution.py:283
  (9 shorter events, 0.1 us)
Async XLA Ops:
  0.0 0.9 copy-start.1
  1.0 1.2 collective-permute-start
  2.3 3.7 %collective-permute-start.1 = (f32[32,128]{1,0:T(8,128)S(1)}, f32[32,128]{1,0:T(8,128)S(1)}, u32[]{:S(2)}, u32[]{:S(2)}) collective-permute-start(f32[32,128]{1,0:T(8,128)S(1)} %add.22), channel_id=1, source_target_pairs={{0,32},{32,0},{64,96},{96,64},{1,33},{33,1},{65,97},{97,65},{2,34}... | collective-permute-start | bytes 49160 | tf_op jit(solution)/shard_map/ppermute | solution.py:301
  6.0 5.7 %collective-permute-start.2 = (f32[32,128]{1,0:T(8,128)S(1)}, f32[32,128]{1,0:T(8,128)S(1)}, u32[]{:S(2)}, u32[]{:S(2)}) collective-permute-start(f32[32,128]{1,0:T(8,128)S(1)} %add.23.moments_ref), channel_id=1, source_target_pairs={{0,64},{32,96},{64,0},{96,32},{1,65},{33,97},{65,1},{97,33},{2,66}... | collective-permute-start | bytes 49160 | tf_op jit(solution)/shard_map/ppermute | solution.py:302
  11.7 0.9 copy-start.2
  12.6 1.8 %copy-start.3 = (bf16[64,2304]{1,0:T(8,128)(2,1)S(1)}, bf16[64,2304]{1,0:T(8,128)(2,1)}, u32[]{:S(2)}) copy-start(bf16[64,2304]{1,0:T(8,128)(2,1)} %param.13) | copy-start | bytes 884740
  14.4 16.4 %collective-permute-start.5 = (bf16[64,2304]{1,0:T(8,128)(2,1)S(1)}, bf16[64,2304]{1,0:T(8,128)(2,1)S(1)}, u32[]{:S(2)}, u32[]{:S(2)}) collective-permute-start(bf16[64,2304]{1,0:T(8,128)(2,1)S(1)} %copy-done.3), channel_id=1, source_target_pairs={{0,64},{32,96},{64,0},{96,32},{1,65},{33,97},{65,1},{97,33},{2,66}... | collective-permute-start | bytes 884744 | tf_op jit(solution)/shard_map/ppermute | solution.py:309
  17.9 12.1 %collective-permute-start.4 = (bf16[64,2304]{1,0:T(8,128)(2,1)S(1)}, bf16[64,2304]{1,0:T(8,128)(2,1)S(1)}, u32[]{:S(2)}, u32[]{:S(2)}) collective-permute-start(bf16[64,2304]{1,0:T(8,128)(2,1)S(1)} %copy-done.3), channel_id=1, source_target_pairs={{0,96},{32,0},{64,32},{96,64},{1,97},{33,1},{65,33},{97,65},{2,98}... | collective-permute-start | bytes 884744 | tf_op jit(solution)/shard_map/ppermute | solution.py:309
  18.6 10.6 %collective-permute-start.3 = (bf16[64,2304]{1,0:T(8,128)(2,1)S(1)}, bf16[64,2304]{1,0:T(8,128)(2,1)S(1)}, u32[]{:S(2)}, u32[]{:S(2)}) collective-permute-start(bf16[64,2304]{1,0:T(8,128)(2,1)S(1)} %copy-done.3), channel_id=1, source_target_pairs={{0,32},{32,64},{64,96},{96,0},{1,33},{33,65},{65,97},{97,1},{2,34}... | collective-permute-start | bytes 884744 | tf_op jit(solution)/shard_map/ppermute | solution.py:309
  19.9 37.4 %all-to-all-start = ((bf16[16,32,2304]{2,1,0:T(8,128)(2,1)}), bf16[16,32,2304]{2,1,0:T(8,128)(2,1)S(1)}, u32[]{:S(2)}, u32[]{:S(2)}) async-start(bf16[16,32,2304]{2,1,0:T(8,128)(2,1)} %normalize.1), calls=%async_computation | async-start | bytes 4718592 | tf_op jit(solution)/shard_map/all_to_all | solution.py:305
  30.0 1.5 %copy-start.4 = (bf16[2304,32]{0,1:T(8,128)(2,1)S(1)}, bf16[2304,32]{0,1:T(8,128)(2,1)}, u32[]{:S(2)}) copy-start(bf16[2304,32]{0,1:T(8,128)(2,1)} %param.11) | copy-start | bytes 442372
  31.5 3.2 %collective-permute-start.6 = (bf16[256,2304]{1,0:T(8,128)(2,1)}, bf16[256,2304]{1,0:T(8,128)(2,1)}, u32[]{:S(2)}, u32[]{:S(2)}) collective-permute-start(bf16[256,2304]{1,0:T(8,128)(2,1)} %constant_dynamic-update-slice_fusion.own_ref), channel_id=1, source_target_pairs={{0,16},{16,0},{1,17},{17,1},{2,18},{18,2},{3,19},{19,3},{4,20},{20... | collective-permute-start | bytes 3538952 | tf_op jit(solution)/shard_map/ppermute | solution.py:311
  62.5 2.0 %collective-permute-start.7 = (bf16[4,8,2,16,256]{4,3,2,1,0:T(8,128)(2,1)S(1)}, bf16[4,8,2,16,256]{4,3,2,1,0:T(8,128)(2,1)S(1)}, u32[]{:S(2)}, u32[]{:S(2)}) collective-permute-start(bf16[4,8,2,16,256]{4,3,2,1,0:T(8,128)(2,1)S(1)} %get-tuple-element.19), channel_id=1, source_target_pairs={{0,16},{16,0},{1,17},{17,1},{2,18},{18,2},{3,19},{19,3},{4,20},{20... | collective-permute-start | bytes 1572872 | tf_op jit(solution)/shard_map/ppermute | solution.py:318
  85.1 27.0 %slice-start = ((s8[4718592]{0:T(1024)(128)(4,1)}), s8[4194304]{0:T(1024)(128)(4,1)S(1)}, s32[]{:S(2)}) async-start(s8[4718592]{0:T(1024)(128)(4,1)} %bitcast.7), calls=%async_computation.4 | async-start | bytes 8388608
  85.1 27.0 %slice-start.1 = ((s8[4718592]{0:T(1024)(128)(4,1)}), s8[524288]{0:T(1024)(128)(4,1)S(1)}, s32[]{:S(2)}) async-start(s8[4718592]{0:T(1024)(128)(4,1)} %bitcast.7), calls=%async_computation.5 | async-start | bytes 1048576
  110.2 1.9 %collective-permute-start.8 = (bf16[4,8,2,16,256]{4,3,2,1,0:T(8,128)(2,1)S(1)}, bf16[4,8,2,16,256]{4,3,2,1,0:T(8,128)(2,1)S(1)}, u32[]{:S(2)}, u32[]{:S(2)}) collective-permute-start(bf16[4,8,2,16,256]{4,3,2,1,0:T(8,128)(2,1)S(1)} %bitcast.11), channel_id=1, source_target_pairs={{0,16},{16,0},{1,17},{17,1},{2,18},{18,2},{3,19},{19,3},{4,20},{20... | collective-permute-start | bytes 1572872 | tf_op jit(solution)/shard_map/ppermute | solution.py:323
  112.1 2.0 %copy-start = (bf16[768,2304]{1,0:T(8,128)(2,1)S(1)}, bf16[768,2304]{1,0:T(8,128)(2,1)}, u32[]{:S(2)}) copy-start(bf16[768,2304]{1,0:T(8,128)(2,1)} %weight_ref.3) | copy-start | bytes 10616836

commit v3 on v2

--- a/solution.py
+++ b/solution.py
@@ -24,7 +24,8 @@
     return lax.broadcasted_iota(jnp.int32, shape, 1) < 4
 
 
-def moments_kernel(residual_ref, out_ref):
+def moments_kernel(residual_ref, out_ref, kept_ref):
+    kept_ref[...] = residual_ref[...]
     values = residual_ref[...].astype(F32)
     sums = jnp.sum(values, axis=1, keepdims=True)
     squares = jnp.sum(values * values, axis=1, keepdims=True)
@@ -35,7 +36,10 @@
 def row_moments(residual):
     return pl.pallas_call(
         moments_kernel,
-        out_shape=jax.ShapeDtypeStruct((residual.shape[0], 128), F32),
+        out_shape=[
+            jax.ShapeDtypeStruct((residual.shape[0], 128), F32),
+            jax.ShapeDtypeStruct(residual.shape, BF16),
+        ],
         compiler_params=pltpu.CompilerParams(vmem_limit_bytes=NARROW),
         name="row_moments",
     )(residual)
@@ -57,32 +61,38 @@
         normalize_kernel,
         out_shape=jax.ShapeDtypeStruct((16, rows, width), BF16),
         compiler_params=pltpu.CompilerParams(vmem_limit_bytes=NARROW),
+        cost_estimate=pl.CostEstimate(flops=1 << 20, bytes_accessed=24 << 20, transcendentals=0),
         name="normalize",
     )(residual, moments, more, gain)
 
 
-def feed_kernel(own_ref, other_ref, weight_ref, out_ref):
-    rows = own_ref.shape[0]
-    weight = weight_ref[...]
-    out_ref[:rows, :] = jnp.dot(own_ref[...], weight, preferred_element_type=F32)
-    out_ref[rows:, :] = jnp.dot(other_ref[...], weight, preferred_element_type=F32)
-
-
-def feed(own, other, weight):
-    rows, depth = own.shape
+def feed_kernel(*refs):
+    hidden_refs, (weight_ref, out_ref, x_ref) = refs[:8], refs[8:]
+
+    @pl.when(pl.program_id(0) + lax.axis_index("c") * 4 % 4 == 0)
+    def _():
+        for i, ref in enumerate(hidden_refs):
+            x_ref[i * 64 : i * 64 + 64, :] = ref[...]
+
+    out_ref[...] = jnp.dot(x_ref[...], weight_ref[...], preferred_element_type=F32)
+
+
+def feed(hidden, weight):
+    rows, depth = 64 * len(hidden), hidden[0].shape[1]
     width = weight.shape[1]
-    tile = 256
-    whole = pl.BlockSpec((rows, depth), lambda i: (0, 0), pipeline_mode=pl.Buffered(1))
+    tile = 768
+    whole = pl.BlockSpec((64, depth), lambda i: (0, 0), pipeline_mode=pl.Buffered(1))
     return pl.pallas_call(
         feed_kernel,
         grid=(width // tile,),
-        in_specs=[whole, whole, pl.BlockSpec((depth, tile), lambda i: (0, i))],
-        out_specs=pl.BlockSpec((2 * rows, tile), lambda i: (0, i)),
-        out_shape=jax.ShapeDtypeStruct((2 * rows, width), F32),
-        compiler_params=pltpu.CompilerParams(vmem_limit_bytes=WIDE),
-        cost_estimate=pl.CostEstimate(flops=1, bytes_accessed=1, transcendentals=0),
+        in_specs=[whole] * len(hidden) + [pl.BlockSpec((depth, tile), lambda i: (0, i))],
+        out_specs=pl.BlockSpec((rows, tile), lambda i: (0, i)),
+        out_shape=jax.ShapeDtypeStruct((rows, width), F32),
+        scratch_shapes=[pltpu.VMEM((rows, depth), BF16)],
+        compiler_params=pltpu.CompilerParams(vmem_limit_bytes=20 << 20),
+        cost_estimate=pl.CostEstimate(flops=1 << 31, bytes_accessed=1, transcendentals=0),
         name="feed",
-    )(own, other, weight)
+    )(*hidden, weight)
 
 
 def project_kernel(x_ref, query_ref, fresh_ref, mine_ref, theirs_ref, slots_ref):
@@ -129,7 +139,7 @@
         out_specs=[pl.BlockSpec(out.shape, lambda i: (0, 0, 0, 0, 0))] * 2,
         out_shape=[out, out],
         scratch_shapes=[pltpu.VMEM((3, rows, HEAD), F32)],
-        compiler_params=pltpu.CompilerParams(vmem_limit_bytes=48 << 20),
+        compiler_params=pltpu.CompilerParams(vmem_limit_bytes=24 << 20),
         cost_estimate=pl.CostEstimate(
             flops=2 * rows * width * 896, bytes_accessed=8 << 20, transcendentals=0
         ),
@@ -137,76 +147,72 @@
     )(x, query_weight, fresh_weight)
 
 
-def attend_kernel(parts_ref, cache_ref, out_ref, held_ref, sums_ref, result_ref, sems):
-    copies = [
-        pltpu.make_async_copy(cache_ref.at[t], held_ref.at[t], sems.at[t]) for t in range(4)
-    ]
-    for copy in copies:
-        copy.start()
-    total = parts_ref[0].astype(F32)
-    for z in range(1, 4):
-        total = total + parts_ref[z].astype(F32)
-    total = total.astype(BF16).astype(F32).reshape(256, HEAD)
-    for half in range(2):
-        sums_ref[half] = total[:, half * 128 : half * 128 + 128]
-        result_ref[half] = jnp.zeros((256, 128), F32)
+def attend_kernel(parts_ref, cache_ref, out_ref, sums_ref, result_ref):
+    t = pl.program_id(0)
+
+    @pl.when(t == 0)
+    def _():
+        total = parts_ref[0].astype(F32)
+        for z in range(1, 4):
+            total = total + parts_ref[z].astype(F32)
+        total = total.astype(BF16).astype(F32).reshape(256, HEAD)
+        for half in range(2):
+            sums_ref[half] = total[:, half * 128 : half * 128 + 128]
+            result_ref[half] = jnp.zeros((256, 128), F32)
+
+    def slot(h):
+        return jnp.concatenate(
+            [sums_ref[half, pl.ds(h * 4 + t, 16, stride=16), :] for half in range(2)], axis=1
+        )
+
+    query = jnp.concatenate([slot(h) for h in range(3)], axis=0)
+    columns = sums_ref[0, pl.ds(12 + t, 16, stride=16), :]
+    fresh = [jnp.sum(columns[4 * b : 4 * b + 4], axis=0, keepdims=True) for b in range(4)]
+    new_key = jnp.concatenate(fresh[:2], axis=1)
+    new_value = jnp.concatenate(fresh[2:], axis=1)
     scale = HEAD ** (-0.5)
-    for t in range(4):
-
-        def slot(h):
-            return jnp.concatenate(
-                [sums_ref[half, pl.ds(h * 4 + t, 16, stride=16), :] for half in range(2)], axis=1
-            )
-
-        query = jnp.concatenate([slot(h) for h in range(3)], axis=0)
-        columns = sums_ref[0, pl.ds(12 + t, 16, stride=16), :]
-        fresh = [jnp.sum(columns[4 * b : 4 * b + 4], axis=0, keepdims=True) for b in range(4)]
-        new_key = jnp.concatenate(fresh[:2], axis=1)
-        new_value = jnp.concatenate(fresh[2:], axis=1)
-        own = jnp.sum(query * new_key, axis=1, keepdims=True) * scale
-        copies[t].wait()
-        scores = (
-            lax.dot_general(
-                query.astype(BF16),
-                held_ref[t, :, :HEAD],
-                (((1,), (1,)), ((), ())),
-                preferred_element_type=F32,
-            )
-            * scale
+    own = jnp.sum(query * new_key, axis=1, keepdims=True) * scale
+    scores = (
+        lax.dot_general(
+            query.astype(BF16),
+            cache_ref[0, :, :HEAD],
+            (((1,), (1,)), ((), ())),
+            preferred_element_type=F32,
         )
-        highest = jnp.maximum(jnp.max(scores, axis=1, keepdims=True), own)
-        e_past = jnp.exp(scores - highest)
-        e_own = jnp.exp(own - highest)
-        total = jnp.sum(e_past, axis=1, keepdims=True) + e_own
-        result = jnp.dot(e_past.astype(BF16), held_ref[t, :, HEAD:], preferred_element_type=F32)
-        result = (result + e_own * new_value) / total
-        for h in range(3):
-            for half in range(2):
-                result_ref[half, pl.ds(h * 4 + t, 16, stride=16), :] = result[
-                    h * 16 : h * 16 + 16, half * 128 : half * 128 + 128
-                ]
-    whole = jnp.concatenate([result_ref[0], result_ref[1]], axis=1)
-    whole = whole.reshape(16, 16, HEAD).astype(BF16)
-    for z in range(4):
-        out_ref[z] = whole
+        * scale
+    )
+    highest = jnp.maximum(jnp.max(scores, axis=1, keepdims=True), own)
+    e_past = jnp.exp(scores - highest)
+    e_own = jnp.exp(own - highest)
+    total = jnp.sum(e_past, axis=1, keepdims=True) + e_own
+    result = jnp.dot(e_past.astype(BF16), cache_ref[0, :, HEAD:], preferred_element_type=F32)
+    result = (result + e_own * new_value) / total
+    for h in range(3):
+        for half in range(2):
+            result_ref[half, pl.ds(h * 4 + t, 16, stride=16), :] = result[
+                h * 16 : h * 16 + 16, half * 128 : half * 128 + 128
+            ]
+
+    @pl.when(t + lax.axis_index("c") * 4 % 4 == 3)
+    def _():
+        whole = jnp.concatenate([result_ref[0], result_ref[1]], axis=1)
+        whole = whole.reshape(16, 16, HEAD).astype(BF16)
+        for z in range(4):
+            out_ref[z] = whole
 
 
 def attend(parts, cache):
     return pl.pallas_call(
         attend_kernel,
+        grid=(4,),
         in_specs=[
-            pl.BlockSpec(memory_space=pltpu.VMEM),
-            pl.BlockSpec(memory_space=pl.ANY),
+            pl.BlockSpec((4, 16, 16, HEAD), lambda t: (0, 0, 0, 0)),
+            pl.BlockSpec((1,) + cache.shape[1:], lambda t: (t, 0, 0)),
         ],
-        out_specs=pl.BlockSpec(memory_space=pltpu.VMEM),
+        out_specs=pl.BlockSpec((4, 16, 16, HEAD), lambda t: (0, 0, 0, 0)),
         out_shape=jax.ShapeDtypeStruct((4, 16, 16, HEAD), BF16),
-        scratch_shapes=[
-            pltpu.VMEM(cache.shape, BF16),
-            pltpu.VMEM((2, 256, 128), F32),
-            pltpu.VMEM((2, 256, 128), F32),
-            pltpu.SemaphoreType.DMA((4,)),
-        ],
-        compiler_params=pltpu.CompilerParams(vmem_limit_bytes=WIDE),
+        scratch_shapes=[pltpu.VMEM((2, 256, 128), F32), pltpu.VMEM((2, 256, 128), F32)],
+        compiler_params=pltpu.CompilerParams(vmem_limit_bytes=12 << 20),
         cost_estimate=pl.CostEstimate(
             flops=4 * 4 * 48 * 2048 * 256, bytes_accessed=10 << 20, transcendentals=1 << 19
         ),
@@ -296,19 +302,18 @@
     place = lax.axis_index(XY)
     rows = 16 * own_rows
 
-    moments = row_moments(residual)
+    moments, kept = row_moments(residual)
     moments = moments + lax.ppermute(moments, "c", SWAP)
     moments = moments + lax.ppermute(moments, "z", [(i, i ^ 1) for i in range(4)])
     more = lax.ppermute(moments, "z", [(i, i ^ 2) for i in range(4)])
-    copies = normalize(residual, moments, more, norm_gain[None, :])
+    copies = normalize(kept, moments, more, norm_gain[None, :])
     copies, ffn_hidden, kv_weight = lax.optimization_barrier((copies, ffn_hidden, kv_weight))
     normed = lax.all_to_all(copies, XY, 0, 0).reshape(rows, width)
 
-    hidden = jnp.concatenate(
-        [ffn_hidden]
-        + [lax.ppermute(ffn_hidden, "z", [(i, (i + k) % 4) for i in range(4)]) for k in (1, 3, 2)]
-    )
-    ffn = feed(hidden, lax.ppermute(hidden, "c", SWAP), down_weight)
+    hidden = [ffn_hidden] + [
+        lax.ppermute(ffn_hidden, "z", [(i, (i + k) % 4) for i in range(4)]) for k in (1, 3, 2)
+    ]
+    ffn = feed(hidden + [lax.ppermute(v, "c", SWAP) for v in hidden], down_weight)
     columns = kv_weight.shape[1]
     mask = jnp.arange(128)[None, :] // columns == place % 4
     fresh_weight = jnp.where(mask, jnp.tile(kv_weight, (1, 128 // columns)), 0)

time: 154 us -> 146 us (0.948)
  Pallas kernels: 32.7 us -> 22.8 us
  waiting for transfers between devices: 21.9 us -> 16 us
  local copies, waits for them, and re-layouts: 7.9 us -> 11.8 us
  blocking collectives: 71.7 us -> 74.2 us
    all_to_all x1, waiting for transfers between devices: 9.84 us -> 0.01 us  [body(): normed = lax.all_to_all(copies, XY, 0, 0).reshape(rows, width)]
    pallas_call x3, Pallas kernels: 20.9 us -> 12.4 us  [the longest x1 8.09 us: feed(): pl.pallas_call(feed_kernel, grid=(width // tile,), in_specs=[whole] * len...]
    ppermute x3, waiting for transfers between devices: 1.56 us -> 7.87 us  [body(): lax.ppermute(ffn_hidden, 'z', [(i, (i + k) % 4) for i in range(4)])]
    unnamed x17 -> x18, local copies, waits for them, and re-layouts: 6.11 us -> 9.08 us
    all_to_all x1, blocking collectives: 20.5 us -> 23.3 us  [body(): parts = lax.all_to_all(paired.reshape(64, 16, HEAD), ZXY, 0, 0)]
    ppermute x1 -> x4, waiting for transfers between devices: 2.76 us -> 0.57 us  [body(): lax.ppermute(v, 'c', SWAP)]
    another operation x2, local copies, waits for them, and re-layouts: 0.34 us -> 2.04 us  [body(): fresh_weight = jnp.where(mask, jnp.tile(kv_weight, (1, 128 // columns)), 0)]
  transfers between devices with their start and end apart: 10 -> 13, of which waited for: 8 -> 9; matrix products, arithmetic and copies ran while one was open for 3% -> 3% of each run, Pallas kernels for 8% -> 6%
where the time goes in v3:
time: 146 us
  blocking collectives  74.2 us (51%)
  Pallas kernels  22.8 us (16%)
  starting transfers between devices  19.4 us (13%)
  waiting for transfers between devices  16 us (11%)
  local copies, waits for them, and re-layouts  11.8 us (8%)
    all_to_all x1, blocking collectives, body(): pieces = lax.all_to_all(terms.reshape(16, own_rows, width), XY, 0, 0)  34.3 us
    all_to_all x1, blocking collectives, body(): parts = lax.all_to_all(paired.reshape(64, 16, HEAD), ZXY, 0, 0)  23.3 us
    all_to_all x1, blocking collectives, body(): lax.all_to_all(attended.reshape(64, 16, HEAD), ZXY, 0, 0)  16.7 us
    unnamed x18, local copies, waits for them, and re-layouts  9.08 us
    pallas_call x1, Pallas kernels, feed(): pl.pallas_call(feed_kernel, grid=(width // tile,), in_specs=[whole] * len...  8.09 us
    ppermute x3, waiting for transfers between devices, body(): lax.ppermute(ffn_hidden, 'z', [(i, (i + k) % 4) for i in range(4)])  7.87 us
    all_to_all x1, starting transfers between devices, body(): normed = lax.all_to_all(copies, XY, 0, 0).reshape(rows, width)  7.03 us
    ppermute x3, starting transfers between devices, body(): lax.ppermute(ffn_hidden, 'z', [(i, (i + k) % 4) for i in range(4)])  5.63 us
  transfers between devices with their start and end apart: 13, of which 9 were waited for; matrix products, arithmetic and copies ran while one was open for 3% of the time, Pallas kernels for 6%

profile of v3, /device:TPU:0, one launch (start us, length us, event | category | flops | bytes accessed | tf_op | source)
XLA Modules:
  0.0 145.7 jit_solution(2388659755279287358)
XLA Ops:
  0.0 0.9 copy-done.5
  0.9 0.1 row_moments.1
  1.0 0.1 collective-permute-start
  1.1 1.2 collective-permute-done
  2.3 2.0 %collective-permute-start.1 = (f32[32,128]{1,0:T(8,128)S(1)}, f32[32,128]{1,0:T(8,128)S(1)}, u32[]{:S(2)}, u32[]{:S(2)}) collective-permute-start(f32[32,128]{1,0:T(8,128)S(1)} %add.22), channel_id=1, source_target_pairs={{0,32},{32,0},{64,96},{96,64},{1,33},{33,1},{65,97},{97,65},{2,34}... | collective-permute-start | bytes 49160 | tf_op jit(solution)/shard_map/ppermute | solution.py:307
  4.3 1.7 %collective-permute-done.1 = f32[32,128]{1,0:T(8,128)S(1)} collective-permute-done((f32[32,128]{1,0:T(8,128)S(1)}, f32[32,128]{1,0:T(8,128)S(1)}, u32[]{:S(2)}, u32[]{:S(2)}) %collective-permute-start.1) | collective-permute-done | bytes 16416 | tf_op jit(solution)/shard_map/ppermute | solution.py:307
  6.0 4.0 %collective-permute-start.2 = (f32[32,128]{1,0:T(8,128)S(1)}, f32[32,128]{1,0:T(8,128)S(1)}, u32[]{:S(2)}, u32[]{:S(2)}) collective-permute-start(f32[32,128]{1,0:T(8,128)S(1)} %add.23.moments_ref), channel_id=1, source_target_pairs={{0,64},{32,96},{64,0},{96,32},{1,65},{33,97},{65,1},{97,33},{2,66}... | collective-permute-start | bytes 49160 | tf_op jit(solution)/shard_map/ppermute | solution.py:308
  10.0 0.7 broadcast_in_dim.16.gain_ref
  10.7 1.0 collective-permute-done.2.more_ref
  11.7 1.7 %normalize.1 = bf16[16,32,2304]{2,1,0:T(8,128)(2,1)} custom-call(bf16[32,2304]{1,0:T(8,128)(2,1)S(1)} %get-tuple-element.15.residual_ref, f32[32,128]{1,0:T(8,128)S(1)} %add.23.moments_ref, f32[32,128]{1,0:T(8,128)S(1)} %collective-permute-done.2.more_ref, f32[1,2304]{1,0:T(1,128)S(1)} %broadcast_in_dim.16.gain_ref), custom_call_target="tpu_custom_call" | custom-call | flops 1048576 | bytes 25165824 | tf_op jit(solution)/shard_map/normalize/pallas_call | solution.py:60
  13.4 7.0 %all-to-all-start = ((bf16[16,32,2304]{2,1,0:T(8,128)(2,1)}), bf16[16,32,2304]{2,1,0:T(8,128)(2,1)S(1)}, u32[]{:S(2)}, u32[]{:S(2)}) async-start(bf16[16,32,2304]{2,1,0:T(8,128)(2,1)} %normalize.1), calls=%async_computation | async-start | bytes 4718592 | tf_op jit(solution)/shard_map/all_to_all | solution.py:311
  20.5 0.0 copy-done.4
  20.5 3.6 %collective-permute-start.5 = (bf16[64,2304]{1,0:T(8,128)(2,1)S(1)}, bf16[64,2304]{1,0:T(8,128)(2,1)S(1)}, u32[]{:S(2)}, u32[]{:S(2)}) collective-permute-start(bf16[64,2304]{1,0:T(8,128)(2,1)S(1)} %copy-done.4), channel_id=1, source_target_pairs={{0,64},{32,96},{64,0},{96,32},{1,65},{33,97},{65,1},{97,33},{2,66}... | collective-permute-start | bytes 884744 | tf_op jit(solution)/shard_map/ppermute | solution.py:314
  24.1 0.7 collective-permute-start.4
  24.8 1.3 collective-permute-start.3
  26.1 0.0 collective-permute-start.6
  26.1 1.0 tile.4
  27.1 1.1 copy.10
  28.2 3.8 %collective-permute-done.5.refs_3_ = bf16[64,2304]{1,0:T(8,128)(2,1)S(1)} collective-permute-done((bf16[64,2304]{1,0:T(8,128)(2,1)S(1)}, bf16[64,2304]{1,0:T(8,128)(2,1)S(1)}, u32[]{:S(2)}, u32[]{:S(2)}) %collective-permute-start.5) | collective-permute-done | bytes 294944 | tf_op jit(solution)/shard_map/ppermute | solution.py:314
  32.0 0.0 collective-permute-start.9
  32.0 4.0 %collective-permute-done.4.refs_2_ = bf16[64,2304]{1,0:T(8,128)(2,1)} collective-permute-done((bf16[64,2304]{1,0:T(8,128)(2,1)S(1)}, bf16[64,2304]{1,0:T(8,128)(2,1)}, u32[]{:S(2)}, u32[]{:S(2)}) %collective-permute-start.4) | collective-permute-done | bytes 294944 | tf_op jit(solution)/shard_map/ppermute | solution.py:314
  36.0 0.0 collective-permute-start.8
  36.0 0.0 collective-permute-done.3.refs_1_
  36.0 0.5 collective-permute-start.7
  36.6 1.1 broadcast_select_fusion.fresh_ref
  37.7 0.0 collective-permute-done.6.refs_4_
  37.7 0.0 collective-permute-done.9.refs_7_
  37.7 0.1 collective-permute-done.8.refs_6_
  37.8 0.4 collective-permute-done.7.refs_5_
  38.3 4.0 %copy-done.1 = bf16[2304,2304]{1,0:T(8,128)(2,1)S(1)} copy-done((bf16[2304,2304]{1,0:T(8,128)(2,1)S(1)}, bf16[2304,2304]{1,0:T(8,128)(2,1)}, u32[]{:S(2)}) %copy-start.1) | copy-done | bytes 10616856
  42.3 8.1 %feed.1.ffn_ref = f32[512,2304]{1,0:T(8,128)S(1)} custom-call(bf16[64,2304]{1,0:T(8,128)(2,1)S(1)} %copy-done.4, bf16[64,2304]{1,0:T(8,128)(2,1)} %collective-permute-done.3.refs_1_, bf16[64,2304]{1,0:T(8,128)(2,1)} %collective-permute-done.4.refs_2_, bf16[64,2304]{1,0:T(8,128)(2,1)S(1)} %collective-permute-done.5.refs_3_, ...), custom_call_target="tpu_custom_call" | custom-call | flops 2147483648 | bytes 1 | tf_op jit(solution)/shard_map/feed/pallas_call | solution.py:85
  50.4 0.0 copy-start
  50.4 2.1 %copy-done = f32[512,2304]{1,0:T(8,128)} copy-done((f32[512,2304]{1,0:T(8,128)}, f32[512,2304]{1,0:T(8,128)S(1)}, u32[]{:S(2)}) %copy-start) | copy-done | bytes 4718616
  52.5 0.0 all-to-all-done
  52.5 2.0 %copy-done.6 = bf16[2304,768]{1,0:T(8,128)(2,1)S(1)} copy-done((bf16[2304,768]{1,0:T(8,128)(2,1)S(1)}, bf16[2304,768]{1,0:T(8,128)(2,1)}, u32[]{:S(2)}) %copy-start.6) | copy-done | bytes 3538968
  54.5 3.7 %project.1 = (bf16[4,8,2,16,256]{4,3,2,1,0:T(8,128)(2,1)S(1)}, bf16[4,8,2,16,256]{4,3,2,1,0:T(8,128)(2,1)S(1)}) custom-call(bf16[512,2304]{1,0:T(8,128)(2,1)S(1)} %bitcast.10, bf16[2304,768]{1,0:T(8,128)(2,1)S(1)} %copy-done.6, bf16[2304,128]{1,0:T(8,128)(2,1)S(1)} %broadcast_select_fusion.fresh_ref), custom_call_target="tpu_custom_call" | custom-call | flops 2113929216 | bytes 8388608 | tf_op jit(solution)/shard_map/project/pallas_call | solution.py:131
  58.2 0.2 collective-permute-start.10
  58.4 1.8 %collective-permute-done.10 = bf16[4,8,2,16,256]{4,3,2,1,0:T(8,128)(2,1)S(1)} collective-permute-done((bf16[4,8,2,16,256]{4,3,2,1,0:T(8,128)(2,1)S(1)}, bf16[4,8,2,16,256]{4,3,2,1,0:T(8,128)(2,1)S(1)}, u32[]{:S(2)}, u32[]{:S(2)}) %collective-permute-start.10) | collective-permute-done | bytes 524320 | tf_op jit(solution)/shard_map/ppermute | solution.py:323
  60.2 0.2 add_convert_fusion
  60.4 23.3 %all_to_all.20 = bf16[64,16,256]{2,1,0:T(8,128)(2,1)S(1)} all-to-all(bf16[64,16,256]{2,1,0:T(8,128)(2,1)S(1)} %bitcast.16), channel_id=1, replica_groups=mesh['z'=4,'c'=2,'x'=4,'y'=4] {'z','x','y'}, dimensions={0} | all-to-all | bytes 1048576 | tf_op jit(solution)/shard_map/all_to_all | solution.py:324
  83.7 4.2 %attend.1 = bf16[4,16,16,256]{3,2,1,0:T(8,128)(2,1)S(1)} custom-call(bf16[4,16,16,256]{3,2,1,0:T(8,128)(2,1)S(1)} %bitcast.13, bf16[4,2048,512]{2,1,0:T(8,128)(2,1)S(1)} %copy-done.2), custom_call_target="tpu_custom_call" | custom-call | flops 402653184 | bytes 10485760 | tf_op jit(solution)/shard_map/attend/pallas_call | solution.py:205
  87.9 16.7 %all_to_all.21 = bf16[64,16,256]{2,1,0:T(8,128)(2,1)S(1)} all-to-all(bf16[64,16,256]{2,1,0:T(8,128)(2,1)S(1)} %bitcast.14), channel_id=1, replica_groups=mesh['z'=4,'c'=2,'x'=4,'y'=4] {'z','x','y'}, dimensions={0} | all-to-all | bytes 1048576 | tf_op jit(solution)/shard_map/all_to_all | solution.py:327
  104.7 0.0 collective-permute-start.11
  104.7 1.9 %collective-permute-done.11.other_ref = bf16[4,8,2,16,256]{4,3,2,1,0:T(8,128)(2,1)S(1)} collective-permute-done((bf16[4,8,2,16,256]{4,3,2,1,0:T(8,128)(2,1)S(1)}, bf16[4,8,2,16,256]{4,3,2,1,0:T(8,128)(2,1)S(1)}, u32[]{:S(2)}, u32[]{:S(2)}) %collective-permute-start.11) | collective-permute-done | bytes 524320 | tf_op jit(solution)/shard_map/ppermute | solution.py:328
  106.6 0.0 slice-done.1
  106.6 3.3 %output.1 = bf16[512,2304]{1,0:T(8,128)(2,1)S(1)} custom-call(bf16[4,8,2,16,256]{4,3,2,1,0:T(8,128)(2,1)S(1)} %bitcast.12, bf16[4,8,2,16,256]{4,3,2,1,0:T(8,128)(2,1)S(1)} %collective-permute-done.11.other_ref, bf16[768,2304]{1,0:T(8,128)(2,1)S(1)} %copy-done.3, f32[512,2304]{1,0:T(8,128)S(1)} %bitcast.8), custom_call_target="tpu_custom_call" | custom-call | flops 1811939328 | bytes 12582912 | tf_op jit(solution)/shard_map/output/pallas_call | solution.py:261
  109.9 34.3 %all_to_all.22.pieces_ref = bf16[16,32,2304]{2,1,0:T(8,128)(2,1)S(1)} all-to-all(bf16[16,32,2304]{2,1,0:T(8,128)(2,1)S(1)} %bitcast.9), channel_id=1, replica_groups=mesh['z'=4,'c'=2,'x'=4,'y'=4] {'x','y'}, dimensions={0} | all-to-all | bytes 4718592 | tf_op jit(solution)/shard_map/all_to_all | solution.py:330
  144.2 1.6 %add_pieces.1 = bf16[32,2304]{1,0:T(8,128)(2,1)} custom-call(bf16[16,32,2304]{2,1,0:T(8,128)(2,1)S(1)} %all_to_all.22.pieces_ref), custom_call_target="tpu_custom_call" | custom-call | tf_op jit(solution)/shard_map/add_pieces/pallas_call | solution.py:289
  (15 shorter events, 0.0 us)
Async XLA Ops:
  0.0 0.9 copy-start.5
  1.0 1.2 collective-permute-start
  2.3 3.7 %collective-permute-start.1 = (f32[32,128]{1,0:T(8,128)S(1)}, f32[32,128]{1,0:T(8,128)S(1)}, u32[]{:S(2)}, u32[]{:S(2)}) collective-permute-start(f32[32,128]{1,0:T(8,128)S(1)} %add.22), channel_id=1, source_target_pairs={{0,32},{32,0},{64,96},{96,64},{1,33},{33,1},{65,97},{97,65},{2,34}... | collective-permute-start | bytes 49160 | tf_op jit(solution)/shard_map/ppermute | solution.py:307
  6.0 5.7 %collective-permute-start.2 = (f32[32,128]{1,0:T(8,128)S(1)}, f32[32,128]{1,0:T(8,128)S(1)}, u32[]{:S(2)}, u32[]{:S(2)}) collective-permute-start(f32[32,128]{1,0:T(8,128)S(1)} %add.23.moments_ref), channel_id=1, source_target_pairs={{0,64},{32,96},{64,0},{96,32},{1,65},{33,97},{65,1},{97,33},{2,66}... | collective-permute-start | bytes 49160 | tf_op jit(solution)/shard_map/ppermute | solution.py:308
  11.7 8.8 %copy-start.4 = (bf16[64,2304]{1,0:T(8,128)(2,1)S(1)}, bf16[64,2304]{1,0:T(8,128)(2,1)}, u32[]{:S(2)}) copy-start(bf16[64,2304]{1,0:T(8,128)(2,1)} %refs_0_) | copy-start | bytes 884740
  13.4 39.1 %all-to-all-start = ((bf16[16,32,2304]{2,1,0:T(8,128)(2,1)}), bf16[16,32,2304]{2,1,0:T(8,128)(2,1)S(1)}, u32[]{:S(2)}, u32[]{:S(2)}) async-start(bf16[16,32,2304]{2,1,0:T(8,128)(2,1)} %normalize.1), calls=%async_computation | async-start | bytes 4718592 | tf_op jit(solution)/shard_map/all_to_all | solution.py:311
  20.5 11.5 %collective-permute-start.5 = (bf16[64,2304]{1,0:T(8,128)(2,1)S(1)}, bf16[64,2304]{1,0:T(8,128)(2,1)S(1)}, u32[]{:S(2)}, u32[]{:S(2)}) collective-permute-start(bf16[64,2304]{1,0:T(8,128)(2,1)S(1)} %copy-done.4), channel_id=1, source_target_pairs={{0,64},{32,96},{64,0},{96,32},{1,65},{33,97},{65,1},{97,33},{2,66}... | collective-permute-start | bytes 884744 | tf_op jit(solution)/shard_map/ppermute | solution.py:314
  24.1 12.0 %collective-permute-start.4 = (bf16[64,2304]{1,0:T(8,128)(2,1)S(1)}, bf16[64,2304]{1,0:T(8,128)(2,1)}, u32[]{:S(2)}, u32[]{:S(2)}) collective-permute-start(bf16[64,2304]{1,0:T(8,128)(2,1)S(1)} %copy-done.4), channel_id=1, source_target_pairs={{0,96},{32,0},{64,32},{96,64},{1,97},{33,1},{65,33},{97,65},{2,98}... | collective-permute-start | bytes 884744 | tf_op jit(solution)/shard_map/ppermute | solution.py:314
  24.8 11.3 %collective-permute-start.3 = (bf16[64,2304]{1,0:T(8,128)(2,1)S(1)}, bf16[64,2304]{1,0:T(8,128)(2,1)}, u32[]{:S(2)}, u32[]{:S(2)}) collective-permute-start(bf16[64,2304]{1,0:T(8,128)(2,1)S(1)} %copy-done.4), channel_id=1, source_target_pairs={{0,32},{32,64},{64,96},{96,0},{1,33},{33,65},{65,97},{97,1},{2,34}... | collective-permute-start | bytes 884744 | tf_op jit(solution)/shard_map/ppermute | solution.py:314
  26.1 11.6 %collective-permute-start.6 = (bf16[64,2304]{1,0:T(8,128)(2,1)S(1)}, bf16[64,2304]{1,0:T(8,128)(2,1)}, u32[]{:S(2)}, u32[]{:S(2)}) collective-permute-start(bf16[64,2304]{1,0:T(8,128)(2,1)S(1)} %copy-done.4), channel_id=1, source_target_pairs={{0,16},{16,0},{1,17},{17,1},{2,18},{18,2},{3,19},{19,3},{4,20},{20... | collective-permute-start | bytes 884744 | tf_op jit(solution)/shard_map/ppermute | solution.py:316
  32.0 5.7 %collective-permute-start.9 = (bf16[64,2304]{1,0:T(8,128)(2,1)S(1)}, bf16[64,2304]{1,0:T(8,128)(2,1)S(1)}, u32[]{:S(2)}, u32[]{:S(2)}) collective-permute-start(bf16[64,2304]{1,0:T(8,128)(2,1)S(1)} %collective-permute-done.5.refs_3_), channel_id=1, source_target_pairs={{0,16},{16,0},{1,17},{17,1},{2,18},{18,2},{3,19},{19,3},{4,20},{20... | collective-permute-start | bytes 884744 | tf_op jit(solution)/shard_map/ppermute | solution.py:316
  36.0 1.8 %collective-permute-start.8 = (bf16[64,2304]{1,0:T(8,128)(2,1)}, bf16[64,2304]{1,0:T(8,128)(2,1)S(1)}, u32[]{:S(2)}, u32[]{:S(2)}) collective-permute-start(bf16[64,2304]{1,0:T(8,128)(2,1)} %collective-permute-done.4.refs_2_), channel_id=1, source_target_pairs={{0,16},{16,0},{1,17},{17,1},{2,18},{18,2},{3,19},{19,3},{4,20},{20... | collective-permute-start | bytes 884744 | tf_op jit(solution)/shard_map/ppermute | solution.py:316
  36.0 2.2 %collective-permute-start.7 = (bf16[64,2304]{1,0:T(8,128)(2,1)}, bf16[64,2304]{1,0:T(8,128)(2,1)S(1)}, u32[]{:S(2)}, u32[]{:S(2)}) collective-permute-start(bf16[64,2304]{1,0:T(8,128)(2,1)} %collective-permute-done.3.refs_1_), channel_id=1, source_target_pairs={{0,16},{16,0},{1,17},{17,1},{2,18},{18,2},{3,19},{19,3},{4,20},{20... | collective-permute-start | bytes 884744 | tf_op jit(solution)/shard_map/ppermute | solution.py:316
  38.3 4.0 %copy-start.1 = (bf16[2304,2304]{1,0:T(8,128)(2,1)S(1)}, bf16[2304,2304]{1,0:T(8,128)(2,1)}, u32[]{:S(2)}) copy-start(bf16[2304,2304]{1,0:T(8,128)(2,1)} %refs_8_.1) | copy-start | bytes 31850500
  50.4 2.1 %copy-start = (f32[512,2304]{1,0:T(8,128)}, f32[512,2304]{1,0:T(8,128)S(1)}, u32[]{:S(2)}) copy-start(f32[512,2304]{1,0:T(8,128)S(1)} %feed.1.ffn_ref) | copy-start | bytes 14155780
  52.5 2.0 %copy-start.6 = (bf16[2304,768]{1,0:T(8,128)(2,1)S(1)}, bf16[2304,768]{1,0:T(8,128)(2,1)}, u32[]{:S(2)}) copy-start(bf16[2304,768]{1,0:T(8,128)(2,1)} %query_ref.1) | copy-start | bytes 10616836
  54.5 29.1 %copy-start.2 = (bf16[4,2048,512]{2,1,0:T(8,128)(2,1)S(1)}, bf16[4,2048,512]{2,1,0:T(8,128)(2,1)}, u32[]{:S(2)}) copy-start(bf16[4,2048,512]{2,1,0:T(8,128)(2,1)} %cache_ref.1) | copy-start | bytes 25165828
  58.2 2.0 %collective-permute-start.10 = (bf16[4,8,2,16,256]{4,3,2,1,0:T(8,128)(2,1)S(1)}, bf16[4,8,2,16,256]{4,3,2,1,0:T(8,128)(2,1)S(1)}, u32[]{:S(2)}, u32[]{:S(2)}) collective-permute-start(bf16[4,8,2,16,256]{4,3,2,1,0:T(8,128)(2,1)S(1)} %get-tuple-element.23), channel_id=1, source_target_pairs={{0,16},{16,0},{1,17},{17,1},{2,18},{18,2},{3,19},{19,3},{4,20},{20... | collective-permute-start | bytes 1572872 | tf_op jit(solution)/shard_map/ppermute | solution.py:323
  83.7 22.9 %slice-start = ((s8[4718592]{0:T(1024)(128)(4,1)}), s8[4194304]{0:T(1024)(128)(4,1)S(1)}, s32[]{:S(2)}) async-start(s8[4718592]{0:T(1024)(128)(4,1)} %bitcast.7), calls=%async_computation.4 | async-start | bytes 8388608
  83.7 22.9 %slice-start.1 = ((s8[4718592]{0:T(1024)(128)(4,1)}), s8[524288]{0:T(1024)(128)(4,1)S(1)}, s32[]{:S(2)}) async-start(s8[4718592]{0:T(1024)(128)(4,1)} %bitcast.7), calls=%async_computation.5 | async-start | bytes 1048576
  83.7 22.9 %copy-start.3 = (bf16[768,2304]{1,0:T(8,128)(2,1)S(1)}, bf16[768,2304]{1,0:T(8,128)(2,1)}, u32[]{:S(2)}) copy-start(bf16[768,2304]{1,0:T(8,128)(2,1)} %weight_ref.1) | copy-start | bytes 10616836
  104.7 1.9 %collective-permute-start.11 = (bf16[4,8,2,16,256]{4,3,2,1,0:T(8,128)(2,1)S(1)}, bf16[4,8,2,16,256]{4,3,2,1,0:T(8,128)(2,1)S(1)}, u32[]{:S(2)}, u32[]{:S(2)}) collective-permute-start(bf16[4,8,2,16,256]{4,3,2,1,0:T(8,128)(2,1)S(1)} %bitcast.11), channel_id=1, source_target_pairs={{0,16},{16,0},{1,17},{17,1},{2,18},{18,2},{3,19},{19,3},{4,20},{20... | collective-permute-start | bytes 1572872 | tf_op jit(solution)/shard_map/ppermute | solution.py:328

commit v4 on v3

--- a/solution.py
+++ b/solution.py
@@ -45,8 +45,11 @@
     )(residual)
 
 
-def normalize_kernel(residual_ref, moments_ref, more_ref, gain_ref, out_ref):
-    moments = moments_ref[...] + more_ref[...]
+def normalize_kernel(residual_ref, *refs):
+    moments_refs, (gain_ref, out_ref) = refs[:4], refs[4:]
+    moments = moments_refs[0][...]
+    for ref in moments_refs[1:]:
+        moments = moments + ref[...]
     mean = moments[:, 0:1] / D
     var = moments[:, 64:65] / D - mean * mean
     values = residual_ref[...].astype(F32)
@@ -55,7 +58,7 @@
         out_ref[i] = normed
 
 
-def normalize(residual, moments, more, gain):
+def normalize(residual, moments, gain):
     rows, width = residual.shape
     return pl.pallas_call(
         normalize_kernel,
@@ -63,7 +66,7 @@
         compiler_params=pltpu.CompilerParams(vmem_limit_bytes=NARROW),
         cost_estimate=pl.CostEstimate(flops=1 << 20, bytes_accessed=24 << 20, transcendentals=0),
         name="normalize",
-    )(residual, moments, more, gain)
+    )(residual, *moments, gain)
 
 
 def feed_kernel(*refs):
@@ -277,21 +280,21 @@
 
 
 def add_kernel(pieces_ref, out_ref):
-    total = pieces_ref[0].astype(F32)
-    for i in range(1, pieces_ref.shape[0]):
-        total = total + pieces_ref[i].astype(F32)
-    out_ref[...] = total.astype(BF16)
+    @pl.loop(0, out_ref.shape[1] // 256)
+    def _(n):
+        columns = pl.ds(pl.multiple_of(n * 256, 256), 256)
+        total = pieces_ref[0, :, columns].astype(F32)
+        for i in range(1, pieces_ref.shape[0]):
+            total = total + pieces_ref[i, :, columns].astype(F32)
+        out_ref[:, columns] = total.astype(BF16)
 
 
 def add_pieces(pieces):
-    count, rows, width = pieces.shape
-    tile = 768
     return pl.pallas_call(
         add_kernel,
-        grid=(width // tile,),
-        in_specs=[pl.BlockSpec((count, rows, tile), lambda i: (0, 0, i))],
-        out_specs=pl.BlockSpec((rows, tile), lambda i: (0, i)),
-        out_shape=jax.ShapeDtypeStruct((rows, width), BF16),
+        in_specs=[pl.BlockSpec(memory_space=pltpu.VMEM)],
+        out_specs=pl.BlockSpec(memory_space=pltpu.VMEM),
+        out_shape=jax.ShapeDtypeStruct(pieces.shape[1:], BF16),
         compiler_params=pltpu.CompilerParams(vmem_limit_bytes=NARROW),
         name="add_pieces",
     )(pieces)
@@ -304,9 +307,10 @@
 
     moments, kept = row_moments(residual)
     moments = moments + lax.ppermute(moments, "c", SWAP)
-    moments = moments + lax.ppermute(moments, "z", [(i, i ^ 1) for i in range(4)])
-    more = lax.ppermute(moments, "z", [(i, i ^ 2) for i in range(4)])
-    copies = normalize(kept, moments, more, norm_gain[None, :])
+    moments = [moments] + [
+        lax.ppermute(moments, "z", [(i, (i + k) % 4) for i in range(4)]) for k in (2, 1, 3)
+    ]
+    copies = normalize(kept, moments, norm_gain[None, :])
     copies, ffn_hidden, kv_weight = lax.optimization_barrier((copies, ffn_hidden, kv_weight))
     normed = lax.all_to_all(copies, XY, 0, 0).reshape(rows, width)
 

time: 146 us -> 146 us (level)
  waiting for transfers between devices: 16 us -> 17.6 us
    ppermute x3, waiting for transfers between devices: 7.87 us -> 9.47 us  [body(): lax.ppermute(ffn_hidden, 'z', [(i, (i + k) % 4) for i in range(4)])]
    ppermute x2 -> x3, starting transfers between devices: 5.96 us -> 5.99 us  [body(): lax.ppermute(moments, 'z', [(i, (i + k) % 4) for i in range(4)])]
  transfers between devices with their start and end apart: 13 -> 14, of which waited for: 9 -> 9; matrix products, arithmetic and copies ran while one was open for 3% -> 3% of each run, Pallas kernels for 6% -> 6%
where the time goes in v4:
time: 146 us; the launch traced here: 145 us
  blocking collectives  74.1 us (51%)
  Pallas kernels  22.2 us (15%)
  starting transfers between devices  18 us (12%)
  waiting for transfers between devices  17.6 us (12%)
  local copies, waits for them, and re-layouts  11.8 us (8%)
    all_to_all x1, blocking collectives, body(): pieces = lax.all_to_all(terms.reshape(16, own_rows, width), XY, 0, 0)  34.3 us
    all_to_all x1, blocking collectives, body(): parts = lax.all_to_all(paired.reshape(64, 16, HEAD), ZXY, 0, 0)  23.1 us
    all_to_all x1, blocking collectives, body(): lax.all_to_all(attended.reshape(64, 16, HEAD), ZXY, 0, 0)  16.7 us
    ppermute x3, waiting for transfers between devices, body(): lax.ppermute(ffn_hidden, 'z', [(i, (i + k) % 4) for i in range(4)])  9.47 us
    unnamed x18, local copies, waits for them, and re-layouts  9.08 us
    pallas_call x1, Pallas kernels, feed(): pl.pallas_call(feed_kernel, grid=(width // tile,), in_specs=[whole] * len...  8.09 us
    all_to_all x1, starting transfers between devices, body(): normed = lax.all_to_all(copies, XY, 0, 0).reshape(rows, width)  7.03 us
    ppermute x3, starting transfers between devices, body(): lax.ppermute(moments, 'z', [(i, (i + k) % 4) for i in range(4)])  5.99 us
  transfers between devices with their start and end apart: 14, of which 9 were waited for; matrix products, arithmetic and copies ran while one was open for 3% of the time, Pallas kernels for 6%

profile of v4, /device:TPU:0, one launch (start us, length us, event | category | flops | bytes accessed | tf_op | source)
XLA Modules:
  0.0 145.1 jit_solution(12260541355595253223)
XLA Ops:
  0.0 0.9 copy-done.5
  0.9 0.1 row_moments.1
  1.0 0.1 collective-permute-start
  1.1 1.2 collective-permute-done
  2.3 4.1 %collective-permute-start.3 = (f32[32,128]{1,0:T(8,128)S(1)}, f32[32,128]{1,0:T(8,128)S(1)}, u32[]{:S(2)}, u32[]{:S(2)}) collective-permute-start(f32[32,128]{1,0:T(8,128)S(1)} %add.19.refs_0_), channel_id=1, source_target_pairs={{0,96},{32,0},{64,32},{96,64},{1,97},{33,1},{65,33},{97,65},{2,98}... | collective-permute-start | bytes 49160 | tf_op jit(solution)/shard_map/ppermute | solution.py:311
  6.4 0.0 collective-permute-start.2
  6.4 1.9 %collective-permute-start.1 = (f32[32,128]{1,0:T(8,128)S(1)}, f32[32,128]{1,0:T(8,128)S(1)}, u32[]{:S(2)}, u32[]{:S(2)}) collective-permute-start(f32[32,128]{1,0:T(8,128)S(1)} %add.19.refs_0_), channel_id=1, source_target_pairs={{0,64},{32,96},{64,0},{96,32},{1,65},{33,97},{65,1},{97,33},{2,66}... | collective-permute-start | bytes 49160 | tf_op jit(solution)/shard_map/ppermute | solution.py:311
  8.2 0.7 broadcast_in_dim.16.refs_4_
  9.0 0.0 collective-permute-done.3.refs_3_
  9.0 2.4 %collective-permute-done.2.refs_2_ = f32[32,128]{1,0:T(8,128)S(1)} collective-permute-done((f32[32,128]{1,0:T(8,128)S(1)}, f32[32,128]{1,0:T(8,128)S(1)}, u32[]{:S(2)}, u32[]{:S(2)}) %collective-permute-start.2) | collective-permute-done | bytes 16416 | tf_op jit(solution)/shard_map/ppermute | solution.py:311
  11.3 0.3 collective-permute-done.1.refs_1_
  11.6 1.8 %normalize.1 = bf16[16,32,2304]{2,1,0:T(8,128)(2,1)} custom-call(bf16[32,2304]{1,0:T(8,128)(2,1)S(1)} %get-tuple-element.15.residual_ref, f32[32,128]{1,0:T(8,128)S(1)} %add.19.refs_0_, f32[32,128]{1,0:T(8,128)S(1)} %collective-permute-done.1.refs_1_, f32[32,128]{1,0:T(8,128)S(1)} %collective-permute-done.2.refs_2_, ...), custom_call_target="tpu_custom_call" | custom-call | flops 1048576 | bytes 25165824 | tf_op jit(solution)/shard_map/normalize/pallas_call | solution.py:63
  13.4 7.0 %all-to-all-start = ((bf16[16,32,2304]{2,1,0:T(8,128)(2,1)}), bf16[16,32,2304]{2,1,0:T(8,128)(2,1)S(1)}, u32[]{:S(2)}, u32[]{:S(2)}) async-start(bf16[16,32,2304]{2,1,0:T(8,128)(2,1)} %normalize.1), calls=%async_computation | async-start | bytes 4718592 | tf_op jit(solution)/shard_map/all_to_all | solution.py:315
  20.4 1.9 %collective-permute-start.6 = (bf16[64,2304]{1,0:T(8,128)(2,1)S(1)}, bf16[64,2304]{1,0:T(8,128)(2,1)S(1)}, u32[]{:S(2)}, u32[]{:S(2)}) collective-permute-start(bf16[64,2304]{1,0:T(8,128)(2,1)S(1)} %copy-done.4), channel_id=1, source_target_pairs={{0,64},{32,96},{64,0},{96,32},{1,65},{33,97},{65,1},{97,33},{2,66}... | collective-permute-start | bytes 884744 | tf_op jit(solution)/shard_map/ppermute | solution.py:318
  22.4 1.5 %collective-permute-start.5 = (bf16[64,2304]{1,0:T(8,128)(2,1)S(1)}, bf16[64,2304]{1,0:T(8,128)(2,1)}, u32[]{:S(2)}, u32[]{:S(2)}) collective-permute-start(bf16[64,2304]{1,0:T(8,128)(2,1)S(1)} %copy-done.4), channel_id=1, source_target_pairs={{0,96},{32,0},{64,32},{96,64},{1,97},{33,1},{65,33},{97,65},{2,98}... | collective-permute-start | bytes 884744 | tf_op jit(solution)/shard_map/ppermute | solution.py:318
  23.8 0.8 collective-permute-start.4
  24.6 0.0 collective-permute-start.7
  24.6 1.0 tile.4
  25.6 1.1 copy.10
  26.7 5.3 %collective-permute-done.6.refs_3_ = bf16[64,2304]{1,0:T(8,128)(2,1)S(1)} collective-permute-done((bf16[64,2304]{1,0:T(8,128)(2,1)S(1)}, bf16[64,2304]{1,0:T(8,128)(2,1)S(1)}, u32[]{:S(2)}, u32[]{:S(2)}) %collective-permute-start.6) | collective-permute-done | bytes 294944 | tf_op jit(solution)/shard_map/ppermute | solution.py:318
  32.0 0.0 collective-permute-start.10
  32.0 4.2 %collective-permute-done.5.refs_2_ = bf16[64,2304]{1,0:T(8,128)(2,1)} collective-permute-done((bf16[64,2304]{1,0:T(8,128)(2,1)S(1)}, bf16[64,2304]{1,0:T(8,128)(2,1)}, u32[]{:S(2)}, u32[]{:S(2)}) %collective-permute-start.5) | collective-permute-done | bytes 294944 | tf_op jit(solution)/shard_map/ppermute | solution.py:318
  36.1 0.0 collective-permute-start.9
  36.1 0.0 collective-permute-done.4.refs_1_
  36.1 0.5 collective-permute-start.8
  36.6 1.1 broadcast_select_fusion.fresh_ref
  37.8 0.0 collective-permute-done.7.refs_4_
  37.8 0.0 collective-permute-done.10.refs_7_
  37.8 0.1 collective-permute-done.9.refs_6_
  37.9 0.4 collective-permute-done.8.refs_5_
  38.4 4.0 %copy-done.1 = bf16[2304,2304]{1,0:T(8,128)(2,1)S(1)} copy-done((bf16[2304,2304]{1,0:T(8,128)(2,1)S(1)}, bf16[2304,2304]{1,0:T(8,128)(2,1)}, u32[]{:S(2)}) %copy-start.1) | copy-done | bytes 10616856
  42.4 8.1 %feed.1.ffn_ref = f32[512,2304]{1,0:T(8,128)S(1)} custom-call(bf16[64,2304]{1,0:T(8,128)(2,1)S(1)} %copy-done.4, bf16[64,2304]{1,0:T(8,128)(2,1)} %collective-permute-done.4.refs_1_, bf16[64,2304]{1,0:T(8,128)(2,1)} %collective-permute-done.5.refs_2_, bf16[64,2304]{1,0:T(8,128)(2,1)S(1)} %collective-permute-done.6.refs_3_, ...), custom_call_target="tpu_custom_call" | custom-call | flops 2147483648 | bytes 1 | tf_op jit(solution)/shard_map/feed/pallas_call | solution.py:88
  50.5 2.1 %copy-done = f32[512,2304]{1,0:T(8,128)} copy-done((f32[512,2304]{1,0:T(8,128)}, f32[512,2304]{1,0:T(8,128)S(1)}, u32[]{:S(2)}) %copy-start) | copy-done | bytes 4718616
  52.6 0.0 all-to-all-done
  52.6 2.0 %copy-done.6 = bf16[2304,768]{1,0:T(8,128)(2,1)S(1)} copy-done((bf16[2304,768]{1,0:T(8,128)(2,1)S(1)}, bf16[2304,768]{1,0:T(8,128)(2,1)}, u32[]{:S(2)}) %copy-start.6) | copy-done | bytes 3538968
  54.6 3.7 %project.1 = (bf16[4,8,2,16,256]{4,3,2,1,0:T(8,128)(2,1)S(1)}, bf16[4,8,2,16,256]{4,3,2,1,0:T(8,128)(2,1)S(1)}) custom-call(bf16[512,2304]{1,0:T(8,128)(2,1)S(1)} %bitcast.10, bf16[2304,768]{1,0:T(8,128)(2,1)S(1)} %copy-done.6, bf16[2304,128]{1,0:T(8,128)(2,1)S(1)} %broadcast_select_fusion.fresh_ref), custom_call_target="tpu_custom_call" | custom-call | flops 2113929216 | bytes 8388608 | tf_op jit(solution)/shard_map/project/pallas_call | solution.py:134
  58.3 0.2 collective-permute-start.11
  58.5 1.8 %collective-permute-done.11 = bf16[4,8,2,16,256]{4,3,2,1,0:T(8,128)(2,1)S(1)} collective-permute-done((bf16[4,8,2,16,256]{4,3,2,1,0:T(8,128)(2,1)S(1)}, bf16[4,8,2,16,256]{4,3,2,1,0:T(8,128)(2,1)S(1)}, u32[]{:S(2)}, u32[]{:S(2)}) %collective-permute-start.11) | collective-permute-done | bytes 524320 | tf_op jit(solution)/shard_map/ppermute | solution.py:327
  60.3 0.2 add_convert_fusion
  60.5 23.1 %all_to_all.20 = bf16[64,16,256]{2,1,0:T(8,128)(2,1)S(1)} all-to-all(bf16[64,16,256]{2,1,0:T(8,128)(2,1)S(1)} %bitcast.16), channel_id=1, replica_groups=mesh['z'=4,'c'=2,'x'=4,'y'=4] {'z','x','y'}, dimensions={0} | all-to-all | bytes 1048576 | tf_op jit(solution)/shard_map/all_to_all | solution.py:328
  83.6 0.0 copy-done.2
  83.6 4.2 %attend.1 = bf16[4,16,16,256]{3,2,1,0:T(8,128)(2,1)S(1)} custom-call(bf16[4,16,16,256]{3,2,1,0:T(8,128)(2,1)S(1)} %bitcast.13, bf16[4,2048,512]{2,1,0:T(8,128)(2,1)S(1)} %copy-done.2), custom_call_target="tpu_custom_call" | custom-call | flops 402653184 | bytes 10485760 | tf_op jit(solution)/shard_map/attend/pallas_call | solution.py:208
  87.8 16.7 %all_to_all.21 = bf16[64,16,256]{2,1,0:T(8,128)(2,1)S(1)} all-to-all(bf16[64,16,256]{2,1,0:T(8,128)(2,1)S(1)} %bitcast.14), channel_id=1, replica_groups=mesh['z'=4,'c'=2,'x'=4,'y'=4] {'z','x','y'}, dimensions={0} | all-to-all | bytes 1048576 | tf_op jit(solution)/shard_map/all_to_all | solution.py:331
  104.6 0.0 collective-permute-start.12
  104.6 1.9 %collective-permute-done.12.other_ref = bf16[4,8,2,16,256]{4,3,2,1,0:T(8,128)(2,1)S(1)} collective-permute-done((bf16[4,8,2,16,256]{4,3,2,1,0:T(8,128)(2,1)S(1)}, bf16[4,8,2,16,256]{4,3,2,1,0:T(8,128)(2,1)S(1)}, u32[]{:S(2)}, u32[]{:S(2)}) %collective-permute-start.12) | collective-permute-done | bytes 524320 | tf_op jit(solution)/shard_map/ppermute | solution.py:332
  106.5 3.3 %output.1 = bf16[512,2304]{1,0:T(8,128)(2,1)S(1)} custom-call(bf16[4,8,2,16,256]{4,3,2,1,0:T(8,128)(2,1)S(1)} %bitcast.12, bf16[4,8,2,16,256]{4,3,2,1,0:T(8,128)(2,1)S(1)} %collective-permute-done.12.other_ref, bf16[768,2304]{1,0:T(8,128)(2,1)S(1)} %copy-done.3, f32[512,2304]{1,0:T(8,128)S(1)} %bitcast.8), custom_call_target="tpu_custom_call" | custom-call | flops 1811939328 | bytes 12582912 | tf_op jit(solution)/shard_map/output/pallas_call | solution.py:264
  109.8 34.3 %all_to_all.22.pieces_ref = bf16[16,32,2304]{2,1,0:T(8,128)(2,1)S(1)} all-to-all(bf16[16,32,2304]{2,1,0:T(8,128)(2,1)S(1)} %bitcast.9), channel_id=1, replica_groups=mesh['z'=4,'c'=2,'x'=4,'y'=4] {'x','y'}, dimensions={0} | all-to-all | bytes 4718592 | tf_op jit(solution)/shard_map/all_to_all | solution.py:334
  144.1 1.0 add_pieces.1
  (16 shorter events, 0.0 us)
Async XLA Ops:
  0.0 0.9 copy-start.5
  1.0 1.2 collective-permute-start
  2.3 6.7 %collective-permute-start.3 = (f32[32,128]{1,0:T(8,128)S(1)}, f32[32,128]{1,0:T(8,128)S(1)}, u32[]{:S(2)}, u32[]{:S(2)}) collective-permute-start(f32[32,128]{1,0:T(8,128)S(1)} %add.19.refs_0_), channel_id=1, source_target_pairs={{0,96},{32,0},{64,32},{96,64},{1,97},{33,1},{65,33},{97,65},{2,98}... | collective-permute-start | bytes 49160 | tf_op jit(solution)/shard_map/ppermute | solution.py:311
  6.4 4.9 %collective-permute-start.2 = (f32[32,128]{1,0:T(8,128)S(1)}, f32[32,128]{1,0:T(8,128)S(1)}, u32[]{:S(2)}, u32[]{:S(2)}) collective-permute-start(f32[32,128]{1,0:T(8,128)S(1)} %add.19.refs_0_), channel_id=1, source_target_pairs={{0,32},{32,64},{64,96},{96,0},{1,33},{33,65},{65,97},{97,1},{2,34}... | collective-permute-start | bytes 49160 | tf_op jit(solution)/shard_map/ppermute | solution.py:311
  6.4 5.2 %collective-permute-start.1 = (f32[32,128]{1,0:T(8,128)S(1)}, f32[32,128]{1,0:T(8,128)S(1)}, u32[]{:S(2)}, u32[]{:S(2)}) collective-permute-start(f32[32,128]{1,0:T(8,128)S(1)} %add.19.refs_0_), channel_id=1, source_target_pairs={{0,64},{32,96},{64,0},{96,32},{1,65},{33,97},{65,1},{97,33},{2,66}... | collective-permute-start | bytes 49160 | tf_op jit(solution)/shard_map/ppermute | solution.py:311
  11.6 8.8 %copy-start.4 = (bf16[64,2304]{1,0:T(8,128)(2,1)S(1)}, bf16[64,2304]{1,0:T(8,128)(2,1)}, u32[]{:S(2)}) copy-start(bf16[64,2304]{1,0:T(8,128)(2,1)} %refs_0_) | copy-start | bytes 884740
  13.4 39.2 %all-to-all-start = ((bf16[16,32,2304]{2,1,0:T(8,128)(2,1)}), bf16[16,32,2304]{2,1,0:T(8,128)(2,1)S(1)}, u32[]{:S(2)}, u32[]{:S(2)}) async-start(bf16[16,32,2304]{2,1,0:T(8,128)(2,1)} %normalize.1), calls=%async_computation | async-start | bytes 4718592 | tf_op jit(solution)/shard_map/all_to_all | solution.py:315
  20.4 11.5 %collective-permute-start.6 = (bf16[64,2304]{1,0:T(8,128)(2,1)S(1)}, bf16[64,2304]{1,0:T(8,128)(2,1)S(1)}, u32[]{:S(2)}, u32[]{:S(2)}) collective-permute-start(bf16[64,2304]{1,0:T(8,128)(2,1)S(1)} %copy-done.4), channel_id=1, source_target_pairs={{0,64},{32,96},{64,0},{96,32},{1,65},{33,97},{65,1},{97,33},{2,66}... | collective-permute-start | bytes 884744 | tf_op jit(solution)/shard_map/ppermute | solution.py:318
  22.4 13.8 %collective-permute-start.5 = (bf16[64,2304]{1,0:T(8,128)(2,1)S(1)}, bf16[64,2304]{1,0:T(8,128)(2,1)}, u32[]{:S(2)}, u32[]{:S(2)}) collective-permute-start(bf16[64,2304]{1,0:T(8,128)(2,1)S(1)} %copy-done.4), channel_id=1, source_target_pairs={{0,96},{32,0},{64,32},{96,64},{1,97},{33,1},{65,33},{97,65},{2,98}... | collective-permute-start | bytes 884744 | tf_op jit(solution)/shard_map/ppermute | solution.py:318
  23.8 12.3 %collective-permute-start.4 = (bf16[64,2304]{1,0:T(8,128)(2,1)S(1)}, bf16[64,2304]{1,0:T(8,128)(2,1)}, u32[]{:S(2)}, u32[]{:S(2)}) collective-permute-start(bf16[64,2304]{1,0:T(8,128)(2,1)S(1)} %copy-done.4), channel_id=1, source_target_pairs={{0,32},{32,64},{64,96},{96,0},{1,33},{33,65},{65,97},{97,1},{2,34}... | collective-permute-start | bytes 884744 | tf_op jit(solution)/shard_map/ppermute | solution.py:318
  24.6 13.2 %collective-permute-start.7 = (bf16[64,2304]{1,0:T(8,128)(2,1)S(1)}, bf16[64,2304]{1,0:T(8,128)(2,1)}, u32[]{:S(2)}, u32[]{:S(2)}) collective-permute-start(bf16[64,2304]{1,0:T(8,128)(2,1)S(1)} %copy-done.4), channel_id=1, source_target_pairs={{0,16},{16,0},{1,17},{17,1},{2,18},{18,2},{3,19},{19,3},{4,20},{20... | collective-permute-start | bytes 884744 | tf_op jit(solution)/shard_map/ppermute | solution.py:320
  32.0 5.8 %collective-permute-start.10 = (bf16[64,2304]{1,0:T(8,128)(2,1)S(1)}, bf16[64,2304]{1,0:T(8,128)(2,1)S(1)}, u32[]{:S(2)}, u32[]{:S(2)}) collective-permute-start(bf16[64,2304]{1,0:T(8,128)(2,1)S(1)} %collective-permute-done.6.refs_3_), channel_id=1, source_target_pairs={{0,16},{16,0},{1,17},{17,1},{2,18},{18,2},{3,19},{19,3},{4,20},{20... | collective-permute-start | bytes 884744 | tf_op jit(solution)/shard_map/ppermute | solution.py:320
  36.1 1.8 %collective-permute-start.9 = (bf16[64,2304]{1,0:T(8,128)(2,1)}, bf16[64,2304]{1,0:T(8,128)(2,1)S(1)}, u32[]{:S(2)}, u32[]{:S(2)}) collective-permute-start(bf16[64,2304]{1,0:T(8,128)(2,1)} %collective-permute-done.5.refs_2_), channel_id=1, source_target_pairs={{0,16},{16,0},{1,17},{17,1},{2,18},{18,2},{3,19},{19,3},{4,20},{20... | collective-permute-start | bytes 884744 | tf_op jit(solution)/shard_map/ppermute | solution.py:320
  36.1 2.2 %collective-permute-start.8 = (bf16[64,2304]{1,0:T(8,128)(2,1)}, bf16[64,2304]{1,0:T(8,128)(2,1)S(1)}, u32[]{:S(2)}, u32[]{:S(2)}) collective-permute-start(bf16[64,2304]{1,0:T(8,128)(2,1)} %collective-permute-done.4.refs_1_), channel_id=1, source_target_pairs={{0,16},{16,0},{1,17},{17,1},{2,18},{18,2},{3,19},{19,3},{4,20},{20... | collective-permute-start | bytes 884744 | tf_op jit(solution)/shard_map/ppermute | solution.py:320
  38.4 4.0 %copy-start.1 = (bf16[2304,2304]{1,0:T(8,128)(2,1)S(1)}, bf16[2304,2304]{1,0:T(8,128)(2,1)}, u32[]{:S(2)}) copy-start(bf16[2304,2304]{1,0:T(8,128)(2,1)} %refs_8_.1) | copy-start | bytes 31850500
  50.5 2.1 %copy-start = (f32[512,2304]{1,0:T(8,128)}, f32[512,2304]{1,0:T(8,128)S(1)}, u32[]{:S(2)}) copy-start(f32[512,2304]{1,0:T(8,128)S(1)} %feed.1.ffn_ref) | copy-start | bytes 14155780
  52.6 2.0 %copy-start.6 = (bf16[2304,768]{1,0:T(8,128)(2,1)S(1)}, bf16[2304,768]{1,0:T(8,128)(2,1)}, u32[]{:S(2)}) copy-start(bf16[2304,768]{1,0:T(8,128)(2,1)} %query_ref.1) | copy-start | bytes 10616836
  54.6 29.0 %copy-start.2 = (bf16[4,2048,512]{2,1,0:T(8,128)(2,1)S(1)}, bf16[4,2048,512]{2,1,0:T(8,128)(2,1)}, u32[]{:S(2)}) copy-start(bf16[4,2048,512]{2,1,0:T(8,128)(2,1)} %cache_ref.1) | copy-start | bytes 25165828
  58.3 2.0 %collective-permute-start.11 = (bf16[4,8,2,16,256]{4,3,2,1,0:T(8,128)(2,1)S(1)}, bf16[4,8,2,16,256]{4,3,2,1,0:T(8,128)(2,1)S(1)}, u32[]{:S(2)}, u32[]{:S(2)}) collective-permute-start(bf16[4,8,2,16,256]{4,3,2,1,0:T(8,128)(2,1)S(1)} %get-tuple-element.23), channel_id=1, source_target_pairs={{0,16},{16,0},{1,17},{17,1},{2,18},{18,2},{3,19},{19,3},{4,20},{20... | collective-permute-start | bytes 1572872 | tf_op jit(solution)/shard_map/ppermute | solution.py:327
  83.6 22.9 %slice-start = ((s8[4718592]{0:T(1024)(128)(4,1)}), s8[4194304]{0:T(1024)(128)(4,1)S(1)}, s32[]{:S(2)}) async-start(s8[4718592]{0:T(1024)(128)(4,1)} %bitcast.7), calls=%async_computation.4 | async-start | bytes 8388608
  83.6 22.9 %slice-start.1 = ((s8[4718592]{0:T(1024)(128)(4,1)}), s8[524288]{0:T(1024)(128)(4,1)S(1)}, s32[]{:S(2)}) async-start(s8[4718592]{0:T(1024)(128)(4,1)} %bitcast.7), calls=%async_computation.5 | async-start | bytes 1048576
  83.6 22.9 %copy-start.3 = (bf16[768,2304]{1,0:T(8,128)(2,1)S(1)}, bf16[768,2304]{1,0:T(8,128)(2,1)}, u32[]{:S(2)}) copy-start(bf16[768,2304]{1,0:T(8,128)(2,1)} %weight_ref.1) | copy-start | bytes 10616836
  104.6 1.9 %collective-permute-start.12 = (bf16[4,8,2,16,256]{4,3,2,1,0:T(8,128)(2,1)S(1)}, bf16[4,8,2,16,256]{4,3,2,1,0:T(8,128)(2,1)S(1)}, u32[]{:S(2)}, u32[]{:S(2)}) collective-permute-start(bf16[4,8,2,16,256]{4,3,2,1,0:T(8,128)(2,1)S(1)} %bitcast.11), channel_id=1, source_target_pairs={{0,16},{16,0},{1,17},{17,1},{2,18},{18,2},{3,19},{19,3},{4,20},{20... | collective-permute-start | bytes 1572872 | tf_op jit(solution)/shard_map/ppermute | solution.py:332

commit v5 on v4

--- a/solution.py
+++ b/solution.py
@@ -83,7 +83,7 @@
 def feed(hidden, weight):
     rows, depth = 64 * len(hidden), hidden[0].shape[1]
     width = weight.shape[1]
-    tile = 768
+    tile = 1152
     whole = pl.BlockSpec((64, depth), lambda i: (0, 0), pipeline_mode=pl.Buffered(1))
     return pl.pallas_call(
         feed_kernel,
@@ -92,7 +92,7 @@
         out_specs=pl.BlockSpec((rows, tile), lambda i: (0, i)),
         out_shape=jax.ShapeDtypeStruct((rows, width), F32),
         scratch_shapes=[pltpu.VMEM((rows, depth), BF16)],
-        compiler_params=pltpu.CompilerParams(vmem_limit_bytes=20 << 20),
+        compiler_params=pltpu.CompilerParams(vmem_limit_bytes=28 << 20),
         cost_estimate=pl.CostEstimate(flops=1 << 31, bytes_accessed=1, transcendentals=0),
         name="feed",
     )(*hidden, weight)

time: 146 us -> 146 us (level)
  no operation moved by 1% of the time
where the time goes in v5:
time: 146 us; the launch traced here: 145 us
  blocking collectives  74.1 us (51%)
  Pallas kernels  22.6 us (15%)
  starting transfers between devices  18 us (12%)
  waiting for transfers between devices  17.6 us (12%)
  local copies, waits for them, and re-layouts  11.8 us (8%)
    all_to_all x1, blocking collectives, body(): pieces = lax.all_to_all(terms.reshape(16, own_rows, width), XY, 0, 0)  34.3 us
    all_to_all x1, blocking collectives, body(): parts = lax.all_to_all(paired.reshape(64, 16, HEAD), ZXY, 0, 0)  23.1 us
    all_to_all x1, blocking collectives, body(): lax.all_to_all(attended.reshape(64, 16, HEAD), ZXY, 0, 0)  16.7 us
    ppermute x3, waiting for transfers between devices, body(): lax.ppermute(ffn_hidden, 'z', [(i, (i + k) % 4) for i in range(4)])  9.47 us
    unnamed x18, local copies, waits for them, and re-layouts  9.08 us
    pallas_call x1, Pallas kernels, feed(): pl.pallas_call(feed_kernel, grid=(width // tile,), in_specs=[whole] * len...  8.46 us
    all_to_all x1, starting transfers between devices, body(): normed = lax.all_to_all(copies, XY, 0, 0).reshape(rows, width)  7.03 us
    ppermute x3, starting transfers between devices, body(): lax.ppermute(moments, 'z', [(i, (i + k) % 4) for i in range(4)])  5.99 us
  transfers between devices with their start and end apart: 14, of which 9 were waited for; matrix products, arithmetic and copies ran while one was open for 3% of the time, Pallas kernels for 6%

profile of v5, /device:TPU:0, one launch (start us, length us, event | category | flops | bytes accessed | tf_op | source)
XLA Modules:
  0.0 145.5 jit_solution(13871174121052003597)
XLA Ops:
  0.0 0.9 copy-done.5
  0.9 0.1 row_moments.1
  1.0 0.1 collective-permute-start
  1.1 1.2 collective-permute-done
  2.3 4.1 %collective-permute-start.3 = (f32[32,128]{1,0:T(8,128)S(1)}, f32[32,128]{1,0:T(8,128)S(1)}, u32[]{:S(2)}, u32[]{:S(2)}) collective-permute-start(f32[32,128]{1,0:T(8,128)S(1)} %add.19.refs_0_), channel_id=1, source_target_pairs={{0,96},{32,0},{64,32},{96,64},{1,97},{33,1},{65,33},{97,65},{2,98}... | collective-permute-start | bytes 49160 | tf_op jit(solution)/shard_map/ppermute | solution.py:311
  6.4 0.0 collective-permute-start.2
  6.4 1.9 %collective-permute-start.1 = (f32[32,128]{1,0:T(8,128)S(1)}, f32[32,128]{1,0:T(8,128)S(1)}, u32[]{:S(2)}, u32[]{:S(2)}) collective-permute-start(f32[32,128]{1,0:T(8,128)S(1)} %add.19.refs_0_), channel_id=1, source_target_pairs={{0,64},{32,96},{64,0},{96,32},{1,65},{33,97},{65,1},{97,33},{2,66}... | collective-permute-start | bytes 49160 | tf_op jit(solution)/shard_map/ppermute | solution.py:311
  8.2 0.7 broadcast_in_dim.16.refs_4_
  9.0 0.0 collective-permute-done.3.refs_3_
  9.0 2.4 %collective-permute-done.2.refs_2_ = f32[32,128]{1,0:T(8,128)S(1)} collective-permute-done((f32[32,128]{1,0:T(8,128)S(1)}, f32[32,128]{1,0:T(8,128)S(1)}, u32[]{:S(2)}, u32[]{:S(2)}) %collective-permute-start.2) | collective-permute-done | bytes 16416 | tf_op jit(solution)/shard_map/ppermute | solution.py:311
  11.3 0.3 collective-permute-done.1.refs_1_
  11.6 1.8 %normalize.1 = bf16[16,32,2304]{2,1,0:T(8,128)(2,1)} custom-call(bf16[32,2304]{1,0:T(8,128)(2,1)S(1)} %get-tuple-element.15.residual_ref, f32[32,128]{1,0:T(8,128)S(1)} %add.19.refs_0_, f32[32,128]{1,0:T(8,128)S(1)} %collective-permute-done.1.refs_1_, f32[32,128]{1,0:T(8,128)S(1)} %collective-permute-done.2.refs_2_, ...), custom_call_target="tpu_custom_call" | custom-call | flops 1048576 | bytes 25165824 | tf_op jit(solution)/shard_map/normalize/pallas_call | solution.py:63
  13.4 7.0 %all-to-all-start = ((bf16[16,32,2304]{2,1,0:T(8,128)(2,1)}), bf16[16,32,2304]{2,1,0:T(8,128)(2,1)S(1)}, u32[]{:S(2)}, u32[]{:S(2)}) async-start(bf16[16,32,2304]{2,1,0:T(8,128)(2,1)} %normalize.1), calls=%async_computation | async-start | bytes 4718592 | tf_op jit(solution)/shard_map/all_to_all | solution.py:315
  20.4 1.9 %collective-permute-start.6 = (bf16[64,2304]{1,0:T(8,128)(2,1)S(1)}, bf16[64,2304]{1,0:T(8,128)(2,1)S(1)}, u32[]{:S(2)}, u32[]{:S(2)}) collective-permute-start(bf16[64,2304]{1,0:T(8,128)(2,1)S(1)} %copy-done.4), channel_id=1, source_target_pairs={{0,64},{32,96},{64,0},{96,32},{1,65},{33,97},{65,1},{97,33},{2,66}... | collective-permute-start | bytes 884744 | tf_op jit(solution)/shard_map/ppermute | solution.py:318
  22.4 1.5 collective-permute-start.5
  23.8 0.8 collective-permute-start.4
  24.6 0.0 collective-permute-start.7
  24.6 1.0 tile.4
  25.6 1.1 copy.10
  26.7 5.3 %collective-permute-done.6.refs_3_ = bf16[64,2304]{1,0:T(8,128)(2,1)S(1)} collective-permute-done((bf16[64,2304]{1,0:T(8,128)(2,1)S(1)}, bf16[64,2304]{1,0:T(8,128)(2,1)S(1)}, u32[]{:S(2)}, u32[]{:S(2)}) %collective-permute-start.6) | collective-permute-done | bytes 294944 | tf_op jit(solution)/shard_map/ppermute | solution.py:318
  32.0 0.0 collective-permute-start.10
  32.0 4.2 %collective-permute-done.5.refs_2_ = bf16[64,2304]{1,0:T(8,128)(2,1)} collective-permute-done((bf16[64,2304]{1,0:T(8,128)(2,1)S(1)}, bf16[64,2304]{1,0:T(8,128)(2,1)}, u32[]{:S(2)}, u32[]{:S(2)}) %collective-permute-start.5) | collective-permute-done | bytes 294944 | tf_op jit(solution)/shard_map/ppermute | solution.py:318
  36.1 0.0 collective-permute-start.9
  36.1 0.0 collective-permute-done.4.refs_1_
  36.1 0.5 collective-permute-start.8
  36.6 1.1 broadcast_select_fusion.fresh_ref
  37.8 0.0 collective-permute-done.7.refs_4_
  37.8 0.0 collective-permute-done.10.refs_7_
  37.8 0.1 collective-permute-done.9.refs_6_
  37.9 0.4 collective-permute-done.8.refs_5_
  38.4 4.0 %copy-done.1 = bf16[2304,2304]{1,0:T(8,128)(2,1)S(1)} copy-done((bf16[2304,2304]{1,0:T(8,128)(2,1)S(1)}, bf16[2304,2304]{1,0:T(8,128)(2,1)}, u32[]{:S(2)}) %copy-start.1) | copy-done | bytes 10616856
  42.4 8.5 %feed.1.ffn_ref = f32[512,2304]{1,0:T(8,128)S(1)} custom-call(bf16[64,2304]{1,0:T(8,128)(2,1)S(1)} %copy-done.4, bf16[64,2304]{1,0:T(8,128)(2,1)} %collective-permute-done.4.refs_1_, bf16[64,2304]{1,0:T(8,128)(2,1)} %collective-permute-done.5.refs_2_, bf16[64,2304]{1,0:T(8,128)(2,1)S(1)} %collective-permute-done.6.refs_3_, ...), custom_call_target="tpu_custom_call" | custom-call | flops 2147483648 | bytes 1 | tf_op jit(solution)/shard_map/feed/pallas_call | solution.py:88
  50.8 2.1 %copy-done = f32[512,2304]{1,0:T(8,128)} copy-done((f32[512,2304]{1,0:T(8,128)}, f32[512,2304]{1,0:T(8,128)S(1)}, u32[]{:S(2)}) %copy-start) | copy-done | bytes 4718616
  53.0 0.0 all-to-all-done
  53.0 2.0 %copy-done.6 = bf16[2304,768]{1,0:T(8,128)(2,1)S(1)} copy-done((bf16[2304,768]{1,0:T(8,128)(2,1)S(1)}, bf16[2304,768]{1,0:T(8,128)(2,1)}, u32[]{:S(2)}) %copy-start.6) | copy-done | bytes 3538968
  55.0 3.7 %project.1 = (bf16[4,8,2,16,256]{4,3,2,1,0:T(8,128)(2,1)S(1)}, bf16[4,8,2,16,256]{4,3,2,1,0:T(8,128)(2,1)S(1)}) custom-call(bf16[512,2304]{1,0:T(8,128)(2,1)S(1)} %bitcast.10, bf16[2304,768]{1,0:T(8,128)(2,1)S(1)} %copy-done.6, bf16[2304,128]{1,0:T(8,128)(2,1)S(1)} %broadcast_select_fusion.fresh_ref), custom_call_target="tpu_custom_call" | custom-call | flops 2113929216 | bytes 8388608 | tf_op jit(solution)/shard_map/project/pallas_call | solution.py:134
  58.7 0.2 collective-permute-start.11
  58.9 1.8 %collective-permute-done.11 = bf16[4,8,2,16,256]{4,3,2,1,0:T(8,128)(2,1)S(1)} collective-permute-done((bf16[4,8,2,16,256]{4,3,2,1,0:T(8,128)(2,1)S(1)}, bf16[4,8,2,16,256]{4,3,2,1,0:T(8,128)(2,1)S(1)}, u32[]{:S(2)}, u32[]{:S(2)}) %collective-permute-start.11) | collective-permute-done | bytes 524320 | tf_op jit(solution)/shard_map/ppermute | solution.py:327
  60.7 0.2 add_convert_fusion
  60.9 23.1 %all_to_all.20 = bf16[64,16,256]{2,1,0:T(8,128)(2,1)S(1)} all-to-all(bf16[64,16,256]{2,1,0:T(8,128)(2,1)S(1)} %bitcast.16), channel_id=1, replica_groups=mesh['z'=4,'c'=2,'x'=4,'y'=4] {'z','x','y'}, dimensions={0} | all-to-all | bytes 1048576 | tf_op jit(solution)/shard_map/all_to_all | solution.py:328
  83.9 0.0 copy-done.2
  83.9 4.2 %attend.1 = bf16[4,16,16,256]{3,2,1,0:T(8,128)(2,1)S(1)} custom-call(bf16[4,16,16,256]{3,2,1,0:T(8,128)(2,1)S(1)} %bitcast.13, bf16[4,2048,512]{2,1,0:T(8,128)(2,1)S(1)} %copy-done.2), custom_call_target="tpu_custom_call" | custom-call | flops 402653184 | bytes 10485760 | tf_op jit(solution)/shard_map/attend/pallas_call | solution.py:208
  88.2 16.7 %all_to_all.21 = bf16[64,16,256]{2,1,0:T(8,128)(2,1)S(1)} all-to-all(bf16[64,16,256]{2,1,0:T(8,128)(2,1)S(1)} %bitcast.14), channel_id=1, replica_groups=mesh['z'=4,'c'=2,'x'=4,'y'=4] {'z','x','y'}, dimensions={0} | all-to-all | bytes 1048576 | tf_op jit(solution)/shard_map/all_to_all | solution.py:331
  104.9 0.0 collective-permute-start.12
  104.9 1.9 %collective-permute-done.12.other_ref = bf16[4,8,2,16,256]{4,3,2,1,0:T(8,128)(2,1)S(1)} collective-permute-done((bf16[4,8,2,16,256]{4,3,2,1,0:T(8,128)(2,1)S(1)}, bf16[4,8,2,16,256]{4,3,2,1,0:T(8,128)(2,1)S(1)}, u32[]{:S(2)}, u32[]{:S(2)}) %collective-permute-start.12) | collective-permute-done | bytes 524320 | tf_op jit(solution)/shard_map/ppermute | solution.py:332
  106.9 3.3 %output.1 = bf16[512,2304]{1,0:T(8,128)(2,1)S(1)} custom-call(bf16[4,8,2,16,256]{4,3,2,1,0:T(8,128)(2,1)S(1)} %bitcast.12, bf16[4,8,2,16,256]{4,3,2,1,0:T(8,128)(2,1)S(1)} %collective-permute-done.12.other_ref, bf16[768,2304]{1,0:T(8,128)(2,1)S(1)} %copy-done.3, f32[512,2304]{1,0:T(8,128)S(1)} %bitcast.8), custom_call_target="tpu_custom_call" | custom-call | flops 1811939328 | bytes 12582912 | tf_op jit(solution)/shard_map/output/pallas_call | solution.py:264
  110.2 34.3 %all_to_all.22.pieces_ref = bf16[16,32,2304]{2,1,0:T(8,128)(2,1)S(1)} all-to-all(bf16[16,32,2304]{2,1,0:T(8,128)(2,1)S(1)} %bitcast.9), channel_id=1, replica_groups=mesh['z'=4,'c'=2,'x'=4,'y'=4] {'x','y'}, dimensions={0} | all-to-all | bytes 4718592 | tf_op jit(solution)/shard_map/all_to_all | solution.py:334
  144.4 1.0 add_pieces.1
  (16 shorter events, 0.0 us)
Async XLA Ops:
  0.0 0.9 copy-start.5
  1.0 1.2 collective-permute-start
  2.3 6.7 %collective-permute-start.3 = (f32[32,128]{1,0:T(8,128)S(1)}, f32[32,128]{1,0:T(8,128)S(1)}, u32[]{:S(2)}, u32[]{:S(2)}) collective-permute-start(f32[32,128]{1,0:T(8,128)S(1)} %add.19.refs_0_), channel_id=1, source_target_pairs={{0,96},{32,0},{64,32},{96,64},{1,97},{33,1},{65,33},{97,65},{2,98}... | collective-permute-start | bytes 49160 | tf_op jit(solution)/shard_map/ppermute | solution.py:311
  6.4 4.9 %collective-permute-start.2 = (f32[32,128]{1,0:T(8,128)S(1)}, f32[32,128]{1,0:T(8,128)S(1)}, u32[]{:S(2)}, u32[]{:S(2)}) collective-permute-start(f32[32,128]{1,0:T(8,128)S(1)} %add.19.refs_0_), channel_id=1, source_target_pairs={{0,32},{32,64},{64,96},{96,0},{1,33},{33,65},{65,97},{97,1},{2,34}... | collective-permute-start | bytes 49160 | tf_op jit(solution)/shard_map/ppermute | solution.py:311
  6.4 5.2 %collective-permute-start.1 = (f32[32,128]{1,0:T(8,128)S(1)}, f32[32,128]{1,0:T(8,128)S(1)}, u32[]{:S(2)}, u32[]{:S(2)}) collective-permute-start(f32[32,128]{1,0:T(8,128)S(1)} %add.19.refs_0_), channel_id=1, source_target_pairs={{0,64},{32,96},{64,0},{96,32},{1,65},{33,97},{65,1},{97,33},{2,66}... | collective-permute-start | bytes 49160 | tf_op jit(solution)/shard_map/ppermute | solution.py:311
  11.6 8.8 %copy-start.4 = (bf16[64,2304]{1,0:T(8,128)(2,1)S(1)}, bf16[64,2304]{1,0:T(8,128)(2,1)}, u32[]{:S(2)}) copy-start(bf16[64,2304]{1,0:T(8,128)(2,1)} %refs_0_) | copy-start | bytes 884740
  13.4 39.6 %all-to-all-start = ((bf16[16,32,2304]{2,1,0:T(8,128)(2,1)}), bf16[16,32,2304]{2,1,0:T(8,128)(2,1)S(1)}, u32[]{:S(2)}, u32[]{:S(2)}) async-start(bf16[16,32,2304]{2,1,0:T(8,128)(2,1)} %normalize.1), calls=%async_computation | async-start | bytes 4718592 | tf_op jit(solution)/shard_map/all_to_all | solution.py:315
  20.4 11.5 %collective-permute-start.6 = (bf16[64,2304]{1,0:T(8,128)(2,1)S(1)}, bf16[64,2304]{1,0:T(8,128)(2,1)S(1)}, u32[]{:S(2)}, u32[]{:S(2)}) collective-permute-start(bf16[64,2304]{1,0:T(8,128)(2,1)S(1)} %copy-done.4), channel_id=1, source_target_pairs={{0,64},{32,96},{64,0},{96,32},{1,65},{33,97},{65,1},{97,33},{2,66}... | collective-permute-start | bytes 884744 | tf_op jit(solution)/shard_map/ppermute | solution.py:318
  22.4 13.8 %collective-permute-start.5 = (bf16[64,2304]{1,0:T(8,128)(2,1)S(1)}, bf16[64,2304]{1,0:T(8,128)(2,1)}, u32[]{:S(2)}, u32[]{:S(2)}) collective-permute-start(bf16[64,2304]{1,0:T(8,128)(2,1)S(1)} %copy-done.4), channel_id=1, source_target_pairs={{0,96},{32,0},{64,32},{96,64},{1,97},{33,1},{65,33},{97,65},{2,98}... | collective-permute-start | bytes 884744 | tf_op jit(solution)/shard_map/ppermute | solution.py:318
  23.8 12.3 %collective-permute-start.4 = (bf16[64,2304]{1,0:T(8,128)(2,1)S(1)}, bf16[64,2304]{1,0:T(8,128)(2,1)}, u32[]{:S(2)}, u32[]{:S(2)}) collective-permute-start(bf16[64,2304]{1,0:T(8,128)(2,1)S(1)} %copy-done.4), channel_id=1, source_target_pairs={{0,32},{32,64},{64,96},{96,0},{1,33},{33,65},{65,97},{97,1},{2,34}... | collective-permute-start | bytes 884744 | tf_op jit(solution)/shard_map/ppermute | solution.py:318
  24.6 13.2 %collective-permute-start.7 = (bf16[64,2304]{1,0:T(8,128)(2,1)S(1)}, bf16[64,2304]{1,0:T(8,128)(2,1)}, u32[]{:S(2)}, u32[]{:S(2)}) collective-permute-start(bf16[64,2304]{1,0:T(8,128)(2,1)S(1)} %copy-done.4), channel_id=1, source_target_pairs={{0,16},{16,0},{1,17},{17,1},{2,18},{18,2},{3,19},{19,3},{4,20},{20... | collective-permute-start | bytes 884744 | tf_op jit(solution)/shard_map/ppermute | solution.py:320
  32.0 5.8 %collective-permute-start.10 = (bf16[64,2304]{1,0:T(8,128)(2,1)S(1)}, bf16[64,2304]{1,0:T(8,128)(2,1)S(1)}, u32[]{:S(2)}, u32[]{:S(2)}) collective-permute-start(bf16[64,2304]{1,0:T(8,128)(2,1)S(1)} %collective-permute-done.6.refs_3_), channel_id=1, source_target_pairs={{0,16},{16,0},{1,17},{17,1},{2,18},{18,2},{3,19},{19,3},{4,20},{20... | collective-permute-start | bytes 884744 | tf_op jit(solution)/shard_map/ppermute | solution.py:320
  36.1 1.8 %collective-permute-start.9 = (bf16[64,2304]{1,0:T(8,128)(2,1)}, bf16[64,2304]{1,0:T(8,128)(2,1)S(1)}, u32[]{:S(2)}, u32[]{:S(2)}) collective-permute-start(bf16[64,2304]{1,0:T(8,128)(2,1)} %collective-permute-done.5.refs_2_), channel_id=1, source_target_pairs={{0,16},{16,0},{1,17},{17,1},{2,18},{18,2},{3,19},{19,3},{4,20},{20... | collective-permute-start | bytes 884744 | tf_op jit(solution)/shard_map/ppermute | solution.py:320
  36.1 2.2 %collective-permute-start.8 = (bf16[64,2304]{1,0:T(8,128)(2,1)}, bf16[64,2304]{1,0:T(8,128)(2,1)S(1)}, u32[]{:S(2)}, u32[]{:S(2)}) collective-permute-start(bf16[64,2304]{1,0:T(8,128)(2,1)} %collective-permute-done.4.refs_1_), channel_id=1, source_target_pairs={{0,16},{16,0},{1,17},{17,1},{2,18},{18,2},{3,19},{19,3},{4,20},{20... | collective-permute-start | bytes 884744 | tf_op jit(solution)/shard_map/ppermute | solution.py:320
  38.4 4.0 %copy-start.1 = (bf16[2304,2304]{1,0:T(8,128)(2,1)S(1)}, bf16[2304,2304]{1,0:T(8,128)(2,1)}, u32[]{:S(2)}) copy-start(bf16[2304,2304]{1,0:T(8,128)(2,1)} %refs_8_.1) | copy-start | bytes 31850500
  50.8 2.1 %copy-start = (f32[512,2304]{1,0:T(8,128)}, f32[512,2304]{1,0:T(8,128)S(1)}, u32[]{:S(2)}) copy-start(f32[512,2304]{1,0:T(8,128)S(1)} %feed.1.ffn_ref) | copy-start | bytes 14155780
  53.0 2.0 %copy-start.6 = (bf16[2304,768]{1,0:T(8,128)(2,1)S(1)}, bf16[2304,768]{1,0:T(8,128)(2,1)}, u32[]{:S(2)}) copy-start(bf16[2304,768]{1,0:T(8,128)(2,1)} %query_ref.1) | copy-start | bytes 10616836
  55.0 29.0 %copy-start.2 = (bf16[4,2048,512]{2,1,0:T(8,128)(2,1)S(1)}, bf16[4,2048,512]{2,1,0:T(8,128)(2,1)}, u32[]{:S(2)}) copy-start(bf16[4,2048,512]{2,1,0:T(8,128)(2,1)} %cache_ref.1) | copy-start | bytes 25165828
  58.7 2.0 %collective-permute-start.11 = (bf16[4,8,2,16,256]{4,3,2,1,0:T(8,128)(2,1)S(1)}, bf16[4,8,2,16,256]{4,3,2,1,0:T(8,128)(2,1)S(1)}, u32[]{:S(2)}, u32[]{:S(2)}) collective-permute-start(bf16[4,8,2,16,256]{4,3,2,1,0:T(8,128)(2,1)S(1)} %get-tuple-element.23), channel_id=1, source_target_pairs={{0,16},{16,0},{1,17},{17,1},{2,18},{18,2},{3,19},{19,3},{4,20},{20... | collective-permute-start | bytes 1572872 | tf_op jit(solution)/shard_map/ppermute | solution.py:327
  83.9 22.9 %slice-start = ((s8[4718592]{0:T(1024)(128)(4,1)}), s8[4194304]{0:T(1024)(128)(4,1)S(1)}, s32[]{:S(2)}) async-start(s8[4718592]{0:T(1024)(128)(4,1)} %bitcast.7), calls=%async_computation.4 | async-start | bytes 8388608
  83.9 22.9 %slice-start.1 = ((s8[4718592]{0:T(1024)(128)(4,1)}), s8[524288]{0:T(1024)(128)(4,1)S(1)}, s32[]{:S(2)}) async-start(s8[4718592]{0:T(1024)(128)(4,1)} %bitcast.7), calls=%async_computation.5 | async-start | bytes 1048576
  83.9 22.9 %copy-start.3 = (bf16[768,2304]{1,0:T(8,128)(2,1)S(1)}, bf16[768,2304]{1,0:T(8,128)(2,1)}, u32[]{:S(2)}) copy-start(bf16[768,2304]{1,0:T(8,128)(2,1)} %weight_ref.1) | copy-start | bytes 10616836
  104.9 1.9 %collective-permute-start.12 = (bf16[4,8,2,16,256]{4,3,2,1,0:T(8,128)(2,1)S(1)}, bf16[4,8,2,16,256]{4,3,2,1,0:T(8,128)(2,1)S(1)}, u32[]{:S(2)}, u32[]{:S(2)}) collective-permute-start(bf16[4,8,2,16,256]{4,3,2,1,0:T(8,128)(2,1)S(1)} %bitcast.11), channel_id=1, source_target_pairs={{0,16},{16,0},{1,17},{17,1},{2,18},{18,2},{3,19},{19,3},{4,20},{20... | collective-permute-start | bytes 1572872 | tf_op jit(solution)/shard_map/ppermute | solution.py:332
